TPU v7x, 32 devices: a whole 2x2x4 slice. The times are simulated.
32 devices in a mesh: wide: 8 (over z, y), tensor: 4 (over x, core).
Axes of the slice: x: 2, y: 2, z: 4, core: 2. Of those that a mesh axis runs over, the one named last changes fastest.
Arguments:
- tokens: bfloat16 [8192, 768], P(('wide', 'tensor')), may hold values from -6 to 6
- cotangent: bfloat16 [8192, 768], P(('wide', 'tensor')), may hold values from -6 to 6
- gate_logits: float32 [8192, 2], P('wide'), may hold values from -4 to 4
- routes: int32 [8192, 2], P('wide'), may hold values from 0 to 7, all different within a row; in each aligned block of 256 rows (0 to 255, 256 to 511, ...) at most 128 rows name the same one
- parents: int32 [8, 13], P('wide'), may hold values from 0 to 12, as said below
- mixing_in: float32 [768, 2304], P(('wide', 'tensor')), may hold values from -0.21875 to 0.21875
- mixing_in_mean: float32 [768, 2304], P(('wide', 'tensor')), may hold values from -512 to 512
- mixing_in_square: float32 [768, 2304], P(('wide', 'tensor')), may hold values from 8192 to 32768
- mixing_out: float32 [768, 768], P(('wide', 'tensor')), may hold values from -1.75 to 1.75
- mixing_out_mean: float32 [768, 768], P(('wide', 'tensor')), may hold values from -80 to 80
- mixing_out_square: float32 [768, 768], P(('wide', 'tensor')), may hold values from 184.32 to 737.28
- norm_gains: float32 [2, 768], P(None, ('wide', 'tensor')), may hold values from 0.5 to 1.5
- norm_gains_mean: float32 [2, 768], P(None, ('wide', 'tensor')), may hold values from -1024 to 1024
- norm_gains_square: float32 [2, 768], P(None, ('wide', 'tensor')), may hold values from 32768 to 131072
- shared_in: float32 [768, 2, 2048], P('wide', None, 'tensor'), may hold values from -0.21875 to 0.21875
- shared_in_mean: float32 [768, 2, 2048], P('wide', None, 'tensor'), may hold values from -192 to 192
- shared_in_square: float32 [768, 2, 2048], P('wide', None, 'tensor'), may hold values from 1003.52 to 4014.08
- shared_out: float32 [2048, 768], P('tensor', 'wide'), may hold values from -0.125 to 0.125
- shared_out_mean: float32 [2048, 768], P('tensor', 'wide'), may hold values from -320 to 320
- shared_out_square: float32 [2048, 768], P('tensor', 'wide'), may hold values from 2949.12 to 11796.48
- expert_in: float32 [8, 768, 2, 2048], P('wide', None, None, 'tensor'), may hold values from -0.21875 to 0.21875
- expert_in_mean: float32 [8, 768, 2, 2048], P('wide', None, None, 'tensor'), may hold values from -48 to 48
- expert_in_square: float32 [8, 768, 2, 2048], P('wide', None, None, 'tensor'), may hold values from 59.1872 to 236.7488
- expert_out: float32 [8, 2048, 768], P('wide', 'tensor'), may hold values from -0.125 to 0.125
- expert_out_mean: float32 [8, 2048, 768], P('wide', 'tensor'), may hold values from -80 to 80
- expert_out_square: float32 [8, 2048, 768], P('wide', 'tensor'), may hold values from 184.32 to 737.28
Outputs:
- mixed: bfloat16 [8192, 768], P(('wide', 'tensor'))
- input_grad: float32 [8192, 768], P(('wide', 'tensor'))
- logit_grad: float32 [8192, 2], P(('wide', 'tensor'))
- mixing_in_mean_new: float32 [768, 2304], P(('wide', 'tensor'))
- mixing_in_square_new: float32 [768, 2304], P(('wide', 'tensor'))
- mixing_in_updated: float32 [768, 2304], P(('wide', 'tensor'))
- mixing_out_mean_new: float32 [768, 768], P(('wide', 'tensor'))
- mixing_out_square_new: float32 [768, 768], P(('wide', 'tensor'))
- mixing_out_updated: float32 [768, 768], P(('wide', 'tensor'))
- norm_gains_mean_new: float32 [2, 768], P(None, ('wide', 'tensor'))
- norm_gains_square_new: float32 [2, 768], P(None, ('wide', 'tensor'))
- norm_gains_updated: float32 [2, 768], P(None, ('wide', 'tensor'))
- shared_in_mean_new: float32 [768, 2, 2048], P('wide', None, 'tensor')
- shared_in_square_new: float32 [768, 2, 2048], P('wide', None, 'tensor')
- shared_in_updated: float32 [768, 2, 2048], P('wide', None, 'tensor')
- shared_out_mean_new: float32 [2048, 768], P('tensor', 'wide')
- shared_out_square_new: float32 [2048, 768], P('tensor', 'wide')
- shared_out_updated: float32 [2048, 768], P('tensor', 'wide')
- expert_in_mean_new: float32 [8, 768, 2, 2048], P('wide', None, None, 'tensor')
- expert_in_square_new: float32 [8, 768, 2, 2048], P('wide', None, None, 'tensor')
- expert_in_updated: float32 [8, 768, 2, 2048], P('wide', None, None, 'tensor')
- expert_out_mean_new: float32 [8, 2048, 768], P('wide', 'tensor')
- expert_out_square_new: float32 [8, 2048, 768], P('wide', 'tensor')
- expert_out_updated: float32 [8, 2048, 768], P('wide', 'tensor')
Inputs may be any that keep to these rules, and one draw needn't show every extreme that they name: `routes`: A token's 2 experts differ; in the rows of one device (aligned blocks of 256 tokens) no expert is named more than 128 times. `parents`: in each tree, entry 0 is 0; 4 of the other segments have parent 0 and each of them is the parent of exactly 2 segments.
All inputs are finite; a program needn't handle non-finite values.
Results may differ from a plain program's by a relative error of at most 0.019.
Values may be sent and summed in bfloat16 or wider, within the bound.
No kernel may reach another device: no remote copies, remote signals or barrier semaphores. Data moves between devices by JAX's collectives and lax.ppermute only.
A program may use at most 256 MiB of HBM per device.

v0:
```python
import math

import jax
import jax.numpy as jnp
from jax import lax
from jax.sharding import PartitionSpec as P

HEAD = 64
TOP = 2
TRUNK = 256
SEG = 64
STEP = 5
SEGS = 13


NORM_EPS = 1e-06
BETA_ONE = 0.5
BETA_TWO = 0.5
ADAM_EPS = 1e-08
DECAY = 0.01
RATES = (0.02, 0.15, 0.3, 0.02, 0.012, 0.02, 0.012)


def for_sending(x):

    def short(part):
        return part.astype(jnp.bfloat16) if part.dtype == jnp.float32 else part

    return jax.tree.map(short, x)


def rms_norm(values, gain):
    factor = lax.rsqrt(jnp.mean(values * values, axis=-1, keepdims=True) + NORM_EPS)
    return values * factor * gain


def rotate(values, position):
    half = values.shape[-1] // 2
    frequency = 10000.0 ** (-jnp.arange(half, dtype=position.dtype) / half)
    angles = position[:, None] * frequency[None, :]
    cosine = jnp.cos(angles)[:, None, :]
    sine_part = jnp.sin(angles)[:, None, :]
    first_half = values[..., :half]
    second_half = values[..., half:]
    return jnp.concatenate(
        [
            first_half * cosine - second_half * sine_part,
            second_half * cosine + first_half * sine_part,
        ],
        axis=-1,
    )


def tree_layout(parent_row, places):
    segment = jnp.where(places < TRUNK, 0, 1 + (places - TRUNK) // SEG)
    seg_start = jnp.where(segment == 0, 0, TRUNK + (segment - 1) * SEG)
    matches = segment[:, None] == jnp.arange(SEGS, dtype=jnp.int32)[None, :]
    upward = jnp.sum(jnp.where(matches, parent_row[None, :], 0), axis=1)
    depth_base = jnp.where(upward == 0, TRUNK, TRUNK + SEG)
    position = jnp.where(segment == 0, places, depth_base + places - seg_start)
    return (segment, upward, position)


def allowed_mask(seg_query, up_query, place_query, seg_key, place_key):
    same_segment = (seg_key[None, :] == seg_query[:, None]) & (
        place_key[None, :] <= place_query[:, None]
    )
    ancestor = (seg_query[:, None] != 0) & (
        (seg_key[None, :] == 0) | (seg_key[None, :] == up_query[:, None])
    )
    return same_segment | ancestor


def merge_heads(stacked):
    moved = jnp.moveaxis(stacked, 0, 1)
    return moved.reshape(moved.shape[0], -1)


def attend_forward(queries, keys_all, values_all, allowed):
    head_count = queries.shape[1]
    head_group = math.gcd(head_count, 4)
    score_scale = 1.0 / math.sqrt(queries.shape[2])

    def one_group(group_index):
        part_query = lax.dynamic_slice_in_dim(queries, group_index * head_group, head_group, 1)
        part_key = lax.dynamic_slice_in_dim(keys_all, group_index * head_group, head_group, 1)
        part_value = lax.dynamic_slice_in_dim(values_all, group_index * head_group, head_group, 1)
        scores = (
            jnp.einsum("qhd,khd->hqk", part_query, part_key, preferred_element_type=jnp.float32)
            * score_scale
        )
        scores = jnp.where(allowed[None], scores, -1e30)
        row_top = jnp.max(scores, axis=-1, keepdims=True)
        shifted = jnp.exp(scores - row_top)
        row_total = jnp.sum(shifted, axis=-1, keepdims=True)
        weights = (shifted / row_total).astype(jnp.bfloat16)
        attended = jnp.einsum(
            "hqk,khd->qhd", weights, part_value, preferred_element_type=jnp.float32
        )
        return (attended, (row_top + jnp.log(row_total))[..., 0])

    parts, log_totals = lax.map(one_group, jnp.arange(head_count // head_group, dtype=jnp.int32))
    return (merge_heads(parts), log_totals)


def attend_backward(queries, keys_all, values_all, allowed, grad_attended, log_totals):
    head_count = queries.shape[1]
    head_group = math.gcd(head_count, 4)
    score_scale = 1.0 / math.sqrt(queries.shape[2])

    def one_group(packed):
        group_index, log_group = packed
        part_query = lax.dynamic_slice_in_dim(queries, group_index * head_group, head_group, 1)
        part_key = lax.dynamic_slice_in_dim(keys_all, group_index * head_group, head_group, 1)
        part_value = lax.dynamic_slice_in_dim(values_all, group_index * head_group, head_group, 1)
        part_grad = lax.dynamic_slice_in_dim(grad_attended, group_index * head_group, head_group, 1)
        scores = (
            jnp.einsum("qhd,khd->hqk", part_query, part_key, preferred_element_type=jnp.float32)
            * score_scale
        )
        scores = jnp.where(allowed[None], scores, -1e30)
        probs = jnp.exp(scores - log_group[..., None])
        grad_weights = jnp.einsum(
            "qhd,khd->hqk", part_grad, part_value, preferred_element_type=jnp.float32
        )
        inner = jnp.sum(probs * grad_weights, axis=-1, keepdims=True)
        grad_scores = (probs * (grad_weights - inner)).astype(jnp.bfloat16)
        grad_query = (
            jnp.einsum("hqk,khd->qhd", grad_scores, part_key, preferred_element_type=jnp.float32)
            * score_scale
        )
        grad_key = (
            jnp.einsum("hqk,qhd->khd", grad_scores, part_query, preferred_element_type=jnp.float32)
            * score_scale
        )
        grad_value = jnp.einsum(
            "hqk,qhd->khd",
            probs.astype(jnp.bfloat16),
            part_grad,
            preferred_element_type=jnp.float32,
        )
        return (grad_query, grad_key, grad_value)

    indices = jnp.arange(head_count // head_group, dtype=jnp.int32)
    parts = lax.map(one_group, (indices, log_totals))
    return (merge_heads(parts[0]), merge_heads(parts[1]), merge_heads(parts[2]))


def swiglu_forward(row_block, w_in, w_out):
    gate_up = jnp.einsum("rd,dcf->rcf", row_block, w_in, preferred_element_type=jnp.float32)
    hidden = (jax.nn.silu(gate_up[:, 0]) * gate_up[:, 1]).astype(jnp.bfloat16)
    branch_out = jnp.dot(hidden, w_out, preferred_element_type=jnp.float32)
    return (gate_up, hidden, branch_out)


def activate(gate_up):
    return jax.nn.silu(gate_up[:, 0]) * gate_up[:, 1]


def swiglu_backward(row_block, gate_up, hidden, grad_branch, w_in, w_out):
    grad_w_out = jnp.einsum("rf,rd->fd", hidden, grad_branch, preferred_element_type=jnp.float32)
    grad_hidden = jnp.einsum("rd,fd->rf", grad_branch, w_out, preferred_element_type=jnp.float32)
    pullback = jax.vjp(activate, gate_up)[1]
    grad_gate_up = pullback(grad_hidden)[0].astype(jnp.bfloat16)
    grad_rows = jnp.einsum("rcf,dcf->rd", grad_gate_up, w_in, preferred_element_type=jnp.float32)
    grad_w_in = jnp.einsum(
        "rd,rcf->dcf", row_block, grad_gate_up, preferred_element_type=jnp.float32
    )
    return (grad_rows, grad_w_in, grad_w_out)


def route_slots(block_routes, expert_count):
    onehot = (block_routes[:, None] == jnp.arange(expert_count, dtype=jnp.int32)[None, :]).astype(
        jnp.int32
    )
    before = jnp.cumsum(onehot, axis=0) - onehot
    return (block_routes, jnp.sum(before * onehot, axis=1))


def route_table(slot_dest, slot_count):
    item_count = slot_dest.shape[0]
    return (
        jnp.full((slot_count,), item_count, jnp.int32)
        .at[slot_dest]
        .set(jnp.arange(item_count, dtype=jnp.int32))
    )


def pick_rows(row_block, index):
    padded = jnp.concatenate(
        [row_block, jnp.zeros((1, row_block.shape[1]), row_block.dtype)], axis=0
    )
    return jnp.take(padded, index, axis=0)


def gather_rows(row_block):
    return lax.all_gather(row_block, "tensor", axis=0, tiled=True)


def sum_rows(terms):
    return jax.tree.map(
        lambda part: part.astype(jnp.float32),
        lax.psum_scatter(for_sending(terms), "tensor", scatter_dimension=0, tiled=True),
    )


def adam_step(weight, mean_old, square_old, gradient, rate):
    mean_new = BETA_ONE * mean_old + (1.0 - BETA_ONE) * gradient
    square_new = BETA_TWO * square_old + (1.0 - BETA_TWO) * gradient * gradient
    mean_hat = mean_new / (1.0 - BETA_ONE**STEP)
    square_hat = square_new / (1.0 - BETA_TWO**STEP)
    updated = weight - rate * (mean_hat / (jnp.sqrt(square_hat) + ADAM_EPS) + DECAY * weight)
    return (mean_new, square_new, updated)


def body(
    tokens,
    cotangent,
    gate_logits,
    routes,
    parents,
    mixing_in,
    mixing_in_mean,
    mixing_in_square,
    mixing_out,
    mixing_out_mean,
    mixing_out_square,
    norm_gains,
    norm_gains_mean,
    norm_gains_square,
    shared_in,
    shared_in_mean,
    shared_in_square,
    shared_out,
    shared_out_mean,
    shared_out_square,
    expert_in,
    expert_in_mean,
    expert_in_square,
    expert_out,
    expert_out_mean,
    expert_out_square,
):
    rows_dev = tokens.shape[0]
    model_width = tokens.shape[1]
    expert_count = lax.axis_size("wide")
    tensor_count = lax.axis_size("tensor")
    tensor_rank = lax.axis_index("tensor")
    tree_length = rows_dev * tensor_count
    capacity = 2 * rows_dev * TOP // expert_count
    head_count = model_width // HEAD
    w_mix_in, w_mix_out, gain_low = (
        lax.all_gather(mixing_in.astype(jnp.bfloat16), ("wide", "tensor"), axis=0, tiled=True),
        lax.all_gather(mixing_out.astype(jnp.bfloat16), ("wide", "tensor"), axis=0, tiled=True),
        lax.all_gather(norm_gains.astype(jnp.bfloat16), ("wide", "tensor"), axis=1, tiled=True),
    )
    gain_pair = gain_low.astype(jnp.float32)
    w_sh_in, w_sh_out = (
        lax.all_gather(shared_in.astype(jnp.bfloat16), "wide", axis=0, tiled=True),
        lax.all_gather(shared_out.astype(jnp.bfloat16), "wide", axis=1, tiled=True),
    )
    w_ex_in = expert_in[0].astype(jnp.bfloat16)
    w_ex_out = expert_out[0].astype(jnp.bfloat16)
    place_all = jnp.arange(tree_length, dtype=jnp.int32)
    place_own = tensor_rank * rows_dev + jnp.arange(rows_dev, dtype=jnp.int32)
    seg_all, up_all, depth_all = tree_layout(parents[0], place_all)
    seg_own, up_own, depth_own = tree_layout(parents[0], place_own)
    allowed = allowed_mask(seg_own, up_own, place_own, seg_all, place_all)
    position = depth_own.astype(jnp.float32)
    own_logits = lax.dynamic_slice_in_dim(gate_logits, tensor_rank * rows_dev, rows_dev, 0)
    input_rows = tokens.astype(jnp.float32)
    normed_one = rms_norm(input_rows, gain_pair[0]).astype(jnp.bfloat16)
    mixed_proj = jnp.dot(normed_one, w_mix_in, preferred_element_type=jnp.float32)
    query_raw = mixed_proj[:, :model_width].reshape(rows_dev, head_count, HEAD)
    key_raw = mixed_proj[:, model_width : 2 * model_width].reshape(rows_dev, head_count, HEAD)
    queries = rotate(query_raw, position).astype(jnp.bfloat16)
    own_kv = jnp.concatenate(
        [
            rotate(key_raw, position).reshape(rows_dev, model_width),
            mixed_proj[:, 2 * model_width :],
        ],
        axis=1,
    ).astype(jnp.bfloat16)
    tree_kv = lax.all_gather(own_kv, "tensor", axis=0, tiled=True)
    keys_all = tree_kv[:, :model_width].reshape(tree_length, head_count, HEAD)
    values_all = tree_kv[:, model_width:].reshape(tree_length, head_count, HEAD)
    attended, log_totals = attend_forward(queries, keys_all, values_all, allowed)
    attended_low = attended.astype(jnp.bfloat16)
    residual = input_rows + jnp.dot(attended_low, w_mix_out, preferred_element_type=jnp.float32)
    normed_two = rms_norm(residual, gain_pair[1]).astype(jnp.bfloat16)
    gates = jax.nn.softmax(own_logits, axis=-1)
    grad_out = cotangent.astype(jnp.float32)

    def move_out(buffer):
        return lax.all_to_all(buffer, "wide", split_axis=0, concat_axis=0, tiled=True)

    def move_back(buffer):
        return lax.all_to_all(
            buffer.astype(jnp.bfloat16), "wide", split_axis=0, concat_axis=0, tiled=True
        ).astype(buffer.dtype)

    flat_routes, slot_ids = jax.vmap(lambda block_routes: route_slots(block_routes, expert_count))(
        routes.reshape(tensor_count, -1)
    )
    slot_dest = (
        flat_routes * (tensor_count * capacity)
        + jnp.arange(tensor_count, dtype=jnp.int32)[:, None] * capacity
        + slot_ids
    ).reshape(-1)
    slot_table = route_table(slot_dest, expert_count * tensor_count * capacity)
    tree_stack = gather_rows(jnp.concatenate([normed_two[:, None], cotangent[:, None]], axis=1))
    shared_rows = tree_stack[:, 0]
    grad_tree = tree_stack[:, 1].astype(jnp.float32)
    gates_tree = jax.nn.softmax(gate_logits, axis=-1)
    received = move_out(
        pick_rows(shared_rows, slot_table // TOP).reshape(expert_count, -1, model_width)
    )
    expert_rows = received.reshape(-1, model_width)
    ex_gate_up, ex_hidden, ex_part = swiglu_forward(expert_rows, w_ex_in, w_ex_out)
    sh_gate_up, sh_hidden, sh_part = swiglu_forward(shared_rows, w_sh_in, w_sh_out)
    returned = move_back(ex_part.reshape(expert_count, -1, model_width)).reshape(-1, model_width)
    per_route = jnp.take(returned, slot_dest, axis=0).reshape(tree_length, TOP, model_width)
    mix_terms = jnp.sum(gates_tree[..., None] * per_route, axis=1) + sh_part
    inner_terms = jnp.sum(grad_tree[:, None, :] * per_route, axis=-1)
    expert_mix, gate_grad = sum_rows((mix_terms, inner_terms))
    combined = residual + expert_mix
    logit_grad = gates * (gate_grad - jnp.sum(gates * gate_grad, axis=-1, keepdims=True))
    grad_routes = (gates[..., None] * grad_out[:, None, :]).astype(jnp.bfloat16)
    grad_shared = grad_out.astype(jnp.bfloat16)[:, None]
    grad_stack = gather_rows(jnp.concatenate([grad_routes, grad_shared], axis=1))
    grad_expert_rows = move_out(
        pick_rows(grad_stack[:, :TOP].reshape(-1, model_width), slot_table).reshape(
            expert_count, -1, model_width
        )
    ).reshape(-1, model_width)
    ex_grad_rows, grad_ex_in, grad_ex_out = swiglu_backward(
        expert_rows, ex_gate_up, ex_hidden, grad_expert_rows, w_ex_in, w_ex_out
    )
    sh_grad_rows, grad_sh_in, grad_sh_out = swiglu_backward(
        shared_rows, sh_gate_up, sh_hidden, grad_stack[:, TOP], w_sh_in, w_sh_out
    )
    back_rows = move_back(ex_grad_rows.reshape(expert_count, -1, model_width)).reshape(
        -1, model_width
    )
    per_route_grad = jnp.take(back_rows, slot_dest, axis=0).reshape(tree_length, TOP, model_width)
    grad_normed_two = sum_rows(jnp.sum(per_route_grad, axis=1) + sh_grad_rows)
    norm_pull = jax.vjp(rms_norm, residual, gain_pair[1])[1]
    grad_res_part, grad_gain_two = norm_pull(grad_normed_two)
    grad_residual = grad_out + grad_res_part
    grad_res_low = grad_residual.astype(jnp.bfloat16)
    grad_mix_out = jnp.einsum(
        "td,te->de", attended_low, grad_res_low, preferred_element_type=jnp.float32
    )
    grad_attended = jnp.einsum(
        "te,de->td", grad_res_low, w_mix_out, preferred_element_type=jnp.float32
    ).astype(jnp.bfloat16)
    grad_query, grad_key_part, grad_value_part = attend_backward(
        queries,
        keys_all,
        values_all,
        allowed,
        grad_attended.reshape(rows_dev, head_count, HEAD),
        log_totals,
    )
    key_sums = lax.psum_scatter(
        jnp.concatenate([grad_key_part, grad_value_part], axis=1).astype(jnp.bfloat16),
        "tensor",
        scatter_dimension=0,
        tiled=True,
    ).astype(jnp.float32)
    rope_pull = jax.vjp(lambda values: rotate(values, position), query_raw)[1]
    grad_query_raw = rope_pull(grad_query.reshape(rows_dev, head_count, HEAD))[0].reshape(
        rows_dev, model_width
    )
    grad_key_raw = rope_pull(key_sums[:, :model_width].reshape(rows_dev, head_count, HEAD))[
        0
    ].reshape(rows_dev, model_width)
    grad_projected = jnp.concatenate(
        [grad_query_raw, grad_key_raw, key_sums[:, model_width:]], axis=1
    ).astype(jnp.bfloat16)
    grad_mix_in = jnp.einsum(
        "td,te->de", normed_one, grad_projected, preferred_element_type=jnp.float32
    )
    grad_normed_one = jnp.einsum(
        "te,de->td", grad_projected, w_mix_in, preferred_element_type=jnp.float32
    )
    first_pull = jax.vjp(rms_norm, input_rows, gain_pair[0])[1]
    grad_input_part, grad_gain_one = first_pull(grad_normed_one)
    input_grad = grad_residual + grad_input_part
    reduced_mix_in, reduced_mix_out, reduced_gains = (
        lax.psum_scatter(grad_mix_in, ("wide", "tensor"), scatter_dimension=0, tiled=True),
        lax.psum_scatter(grad_mix_out, ("wide", "tensor"), scatter_dimension=0, tiled=True),
        lax.psum_scatter(
            jnp.stack([grad_gain_one, grad_gain_two]),
            ("wide", "tensor"),
            scatter_dimension=1,
            tiled=True,
        ),
    )
    reduced_sh_in, reduced_sh_out = (
        lax.psum_scatter(
            grad_sh_in.astype(jnp.bfloat16), "wide", scatter_dimension=0, tiled=True
        ).astype(jnp.float32),
        lax.psum_scatter(
            grad_sh_out.astype(jnp.bfloat16), "wide", scatter_dimension=1, tiled=True
        ).astype(jnp.float32),
    )
    weights = (mixing_in, mixing_out, norm_gains, shared_in, shared_out, expert_in, expert_out)
    means = (
        mixing_in_mean,
        mixing_out_mean,
        norm_gains_mean,
        shared_in_mean,
        shared_out_mean,
        expert_in_mean,
        expert_out_mean,
    )
    squares = (
        mixing_in_square,
        mixing_out_square,
        norm_gains_square,
        shared_in_square,
        shared_out_square,
        expert_in_square,
        expert_out_square,
    )
    gradients = (
        reduced_mix_in,
        reduced_mix_out,
        reduced_gains,
        reduced_sh_in,
        reduced_sh_out,
        grad_ex_in[None],
        grad_ex_out[None],
    )
    results = [combined.astype(jnp.bfloat16), input_grad, logit_grad]
    for number in range(7):
        results.extend(
            adam_step(
                weights[number], means[number], squares[number], gradients[number], RATES[number]
            )
        )
    return tuple(results)


def solution(mesh):
    placed = (
        P(("wide", "tensor"), None),
        P(("wide", "tensor"), None),
        P("wide", None),
        P("wide", None),
        P("wide", None),
        P(("wide", "tensor"), None),
        P(("wide", "tensor"), None),
        P(("wide", "tensor"), None),
        P(("wide", "tensor"), None),
        P(("wide", "tensor"), None),
        P(("wide", "tensor"), None),
        P(None, ("wide", "tensor")),
        P(None, ("wide", "tensor")),
        P(None, ("wide", "tensor")),
        P("wide", None, "tensor"),
        P("wide", None, "tensor"),
        P("wide", None, "tensor"),
        P("tensor", "wide"),
        P("tensor", "wide"),
        P("tensor", "wide"),
        P("wide", None, None, "tensor"),
        P("wide", None, None, "tensor"),
        P("wide", None, None, "tensor"),
        P("wide", "tensor", None),
        P("wide", "tensor", None),
        P("wide", "tensor", None),
    )
    return jax.shard_map(
        body,
        mesh=mesh,
        in_specs=placed,
        out_specs=(
            P(("wide", "tensor"), None),
            P(("wide", "tensor"), None),
            P(("wide", "tensor"), None),
            P(("wide", "tensor"), None),
            P(("wide", "tensor"), None),
            P(("wide", "tensor"), None),
            P(("wide", "tensor"), None),
            P(("wide", "tensor"), None),
            P(("wide", "tensor"), None),
            P(None, ("wide", "tensor")),
            P(None, ("wide", "tensor")),
            P(None, ("wide", "tensor")),
            P("wide", None, "tensor"),
            P("wide", None, "tensor"),
            P("wide", None, "tensor"),
            P("tensor", "wide"),
            P("tensor", "wide"),
            P("tensor", "wide"),
            P("wide", None, None, "tensor"),
            P("wide", None, None, "tensor"),
            P("wide", None, None, "tensor"),
            P("wide", "tensor", None),
            P("wide", "tensor", None),
            P("wide", "tensor", None),
        ),
        check_vma=False,
    )
```

profile of v0, /device:TPU:3, one launch (start us, length us, event | category | flops | bytes accessed | tf_op | source)
XLA Modules:
  0.0 1592.9 jit_solution(8599847730845054766)
XLA Ops:
  10.4 37.5 %all-gather = bf16[32,24,2]{1,2,0:T(2,128)(2,1)S(1)} all-gather(bf16[1,24,2]{1,2,0:T(2,128)(2,1)S(1)} %convert_bitcast_fusion.2), channel_id=1, replica_groups=mesh['wide'=8,'tensor'=4] {'wide','tensor'}, dimensions={0}, use_global_device_ids=true | all-gather | bytes 3168 | tf_op jit(solution)/shard_map/all_gather | solution.py:255
  51.0 23.1 %all-gather.8.cloned.1.call-done = bf16[768,2304]{1,0:T(8,128)(2,1)} async-done(((bf16[24,2304]{1,0:T(8,128)(2,1)}), bf16[768,2304]{1,0:T(8,128)(2,1)}) %all-gather.8.cloned.1.call-update) | async-done | bytes 3538960 | tf_op jit(solution)/shard_map/all_gather | solution.py:253
  82.4 23.6 %all-gather.10.cloned.1.call-done = bf16[1024,1536]{1,0:T(8,128)(2,1)} async-done(((bf16[256,1536]{1,0:T(8,128)(2,1)}), bf16[1024,1536]{1,0:T(8,128)(2,1)}) %all-gather.10.cloned.1.call-update) | async-done | bytes 3145744 | tf_op jit(solution)/shard_map/all_gather | solution.py:284
  112.2 24.2 %while.30 = (s32[]{:T(128)}, bf16[3,256,4,64]{1,3,2,0:T(8,128)(2,1)}, f32[3,4,256]{2,1,0:T(4,128)}, s32[3]{0:T(128)}, bf16[1024,12,64]{0,2,1:T(8,128)(2,1)S(1)},...) while((s32[]{:T(128)}, ...), condition=%wide.region_5.6_spmd.clone.clone, body=%wide.region_2.5_spmd.clone.sunk.clone | while | flops 282852352 | bytes 15116739 | solution.py:102
  136.4 28.2 %all-gather.12.cloned.1.call-done = bf16[768,768]{1,0:T(8,128)(2,1)} async-done(((bf16[24,768]{1,0:T(8,128)(2,1)}), bf16[768,768]{1,0:T(8,128)(2,1)}) %all-gather.12.cloned.1.call-update) | async-done | bytes 1179664 | tf_op jit(solution)/shard_map/all_gather | solution.py:254
  199.9 17.8 %gather_fusion = bf16[4096,768]{1,0:T(8,128)(2,1)} fusion(bf16[1025,768]{1,0:T(8,128)(2,1)S(1)} %concatenate.36, s32[4096]{0:T(1024)S(1)} %get-tuple-element.482), kind=kCustom, calls=%fused_computation.2 | custom fusion | bytes 12599296 | tf_op jit(solution)/shard_map/jit(_take)/gather | solution.py:193
  233.5 134.5 %all-to-all-done = bf16[8,512,768]{2,1,0:T(8,128)(2,1)} async-done(((bf16[8,512,768]{2,1,0:T(8,128)(2,1)}), bf16[8,512,768]{2,1,0:T(8,128)(2,1)}, u32[]{:S(2)}, u32[]{:S(2)}) %all-to-all-start) | async-done | bytes 6291488 | tf_op jit(solution)/shard_map/all_to_all | solution.py:295
  411.8 121.1 %all-to-all-done.1 = bf16[8,512,768]{2,1,0:T(8,128)(2,1)} async-done(((bf16[8,512,768]{2,1,0:T(8,128)(2,1)}), bf16[8,512,768]{2,1,0:T(8,128)(2,1)}, u32[]{:S(2)}, u32[]{:S(2)}) %all-to-all-start.1) | async-done | bytes 6291488 | tf_op jit(solution)/shard_map/all_to_all | solution.py:298
  565.6 19.4 %reduce-scatter.16.cloned.1.call-done = bf16[256,2]{1,0:T(8,128)(2,1)} async-done(((bf16[1024,2]{1,0:T(8,128)(2,1)}), bf16[256,2]{1,0:T(8,128)(2,1)}) %reduce-scatter.16.cloned.1.call-update) | async-done | bytes 1040 | tf_op jit(solution)/shard_map/reduce_scatter | solution.py:203
  588.0 37.9 %all-gather.18.cloned.1.call-done = bf16[1024,3,768]{2,0,1:T(8,128)(2,1)} async-done(((bf16[256,3,768]{2,0,1:T(8,128)(2,1)}), bf16[1024,3,768]{2,0,1:T(8,128)(2,1)}) %all-gather.18.cloned.1.call-update) | async-done | bytes 4718608 | tf_op jit(solution)/shard_map/all_gather | solution.py:197
  635.9 17.8 %gather_fusion.1 = bf16[4096,768]{1,0:T(8,128)(2,1)} fusion(bf16[2049,768]{1,0:T(8,128)(2,1)S(1)} %concatenate.38, s32[4096]{0:T(1024)S(1)} %copy-done.55), kind=kCustom, calls=%fused_computation.3 | custom fusion | bytes 12599296 | tf_op jit(solution)/shard_map/jit(_take)/gather | solution.py:193
  657.6 143.0 %all_to_all.20 = bf16[8,512,768]{2,1,0:T(8,128)(2,1)} all-to-all(bf16[8,512,768]{2,1,0:T(8,128)(2,1)S(1)} %broadcast_select_fusion), channel_id=1, replica_groups=mesh['wide'=8,'tensor'=4] {'wide'}, dimensions={0} | all-to-all | bytes 12582912 | tf_op jit(solution)/shard_map/all_to_all | solution.py:295
  800.7 18.5 %fusion.58 = (f32[4096,1,512]{2,0,1:T(8,128)S(1)}, f32[4096,1,512]{2,0,1:T(8,128)}) fusion(f32[4096,2,512]{2,0,1:T(8,128)} %copy-done.2, bf16[4096,768]{1,0:T(8,128)(2,1)} %bitcast.285, f32[1,512,768]{2,1,0:T(8,128)S(1)} %copy-done.72), kind=kOutput, calls=%fused_computation.75 | convolution fusion | flops 3246784512 | bytes 41418752 | tf_op jit(solution)/shard_map/rd,fd->rf/dot_general | solution.py:162
  841.8 130.8 %all-gather.16.cloned.1.call-done = bf16[768,2,512]{2,0,1:T(8,128)(2,1)} async-done(((bf16[96,2,512]{2,0,1:T(8,128)(2,1)}), bf16[768,2,512]{2,0,1:T(8,128)(2,1)}) %all-gather.16.cloned.1.call-update) | async-done | bytes 1572880 | tf_op jit(solution)/shard_map/all_gather | solution.py:259
  981.5 60.9 %reduce-scatter.24.cloned.1.call-done = bf16[512,96]{0,1:T(8,128)(2,1)} async-done(((bf16[512,768]{0,1:T(8,128)(2,1)}), bf16[512,96]{0,1:T(8,128)(2,1)}) %reduce-scatter.24.cloned.1.call-update) | async-done | bytes 98320 | tf_op jit(solution)/shard_map/reduce_scatter | solution.py:404
  1044.2 26.6 %all_gather.30 = bf16[512,768]{0,1:T(8,128)(2,1)S(1)} all-gather(bf16[512,96]{0,1:T(8,128)(2,1)S(1)} %get-tuple-element.474), channel_id=1, replica_groups=mesh['wide'=8,'tensor'=4] {'wide'}, dimensions={1}, use_global_device_ids=true | all-gather | bytes 884736 | tf_op jit(solution)/shard_map/all_gather | solution.py:260
  1139.5 31.2 %multiply_reduce_fusion.2 = f32[1024,768]{1,0:T(8,128)S(1)} fusion(f32[1024,2,768]{2,1,0:T(2,128)} %reshape.448, f32[1024,2]{1,0:T(8,128)S(1)} %copy.196), kind=kLoop, calls=%fused_computation.80 | loop fusion | flops 2359296 | bytes 9445376 | tf_op jit(solution)/shard_map/reduce_sum | solution.py:323
  1175.8 31.1 %reduce-scatter.10.cloned.1.call-done = bf16[256,768]{1,0:T(8,128)(2,1)} async-done(((bf16[1024,768]{1,0:T(8,128)(2,1)}), bf16[256,768]{1,0:T(8,128)(2,1)}) %reduce-scatter.10.cloned.1.call-update) | async-done | bytes 393232 | tf_op jit(solution)/shard_map/reduce_scatter | solution.py:203
  1210.1 34.5 %while.31 = (s32[]{:T(128)}, f32[3,256,4,64]{1,3,2,0:T(8,128)}, bf16[3,1024,4,64]{1,3,2,0:T(8,128)(2,1)}, bf16[3,1024,4,64]{1,3,2,0:T(8,128)(2,1)}, s32[3]{0:T(1...) while((s32[]{:T(128)}, f32[3,256,4,64]{1,3,2,0:T(8,128)}, ...), condition=%wide.region_22.24_spmd.clone.clone, body=%wide.region_20.23_spmd.clone.sunk.clone | while | flops 688978944 | bytes 49590872 | solution.py:145
  1257.1 29.4 %reduce-scatter.14.cloned.1.call-done = bf16[256,1536]{0,1:T(8,128)(2,1)} async-done(((bf16[1024,1536]{0,1:T(8,128)(2,1)}), bf16[256,1536]{0,1:T(8,128)(2,1)}) %reduce-scatter.14.cloned.1.call-update) | async-done | bytes 786448 | tf_op jit(solution)/shard_map/reduce_scatter | solution.py:365
  1294.8 60.7 %reduce-scatter.22.cloned.1.call-done = bf16[96,2,512]{2,0,1:T(8,128)(2,1)} async-done(((bf16[768,2,512]{2,0,1:T(8,128)(2,1)}), bf16[96,2,512]{2,0,1:T(8,128)(2,1)}) %reduce-scatter.22.cloned.1.call-update) | async-done | bytes 196624 | tf_op jit(solution)/shard_map/reduce_scatter | solution.py:401
  1394.5 63.9 %reduce-scatter.20.cloned.1.call-done = f32[24,768]{1,0:T(8,128)} async-done(((f32[768,768]{1,0:T(8,128)}), f32[24,768]{1,0:T(8,128)}) %reduce-scatter.20.cloned.1.call-update) | async-done | bytes 73744 | tf_op jit(solution)/shard_map/reduce_scatter | solution.py:392
  1463.3 40.8 %all-reduce.10 = f32[2,768]{1,0:T(2,128)S(1)} all-reduce(f32[2,768]{1,0:T(2,128)S(1)} %pad_maximum_fusion.9), channel_id=8, replica_groups=mesh['wide'=8,'tensor'=4] {'wide','tensor'}, use_global_device_ids=true, to_apply=%region_32.34.clone | all-reduce | flops 1536 | bytes 12288
  1505.9 77.0 %reduce-scatter.18.cloned.1.call-done = f32[24,2304]{1,0:T(8,128)} async-done(((f32[768,2304]{1,0:T(8,128)}), f32[24,2304]{1,0:T(8,128)}) %reduce-scatter.18.cloned.1.call-update) | async-done | bytes 221200 | tf_op jit(solution)/shard_map/reduce_scatter | solution.py:391
  (405 shorter events, 396.5 us)
Async XLA Ops:
  8.0 66.1 %all-gather.8.cloned.1.call-start = ((), (), s32[]{:S(2)}) async-start(), calls=%async_computation.12 | async-start | bytes 3649536 | tf_op jit(solution)/shard_map/all_gather | solution.py:253
  9.7 96.2 %all-gather.10.cloned.1.call-start = ((), (), s32[]{:S(2)}) async-start(), calls=%async_computation.13 | async-start | bytes 3932160 | tf_op jit(solution)/shard_map/all_gather | solution.py:284
  79.6 85.1 %all-gather.12.cloned.1.call-start = ((), (), s32[]{:S(2)}) async-start(), calls=%async_computation.14 | async-start | bytes 1216512 | tf_op jit(solution)/shard_map/all_gather | solution.py:254
  80.3 115.6 %all-gather.14.cloned.1.call-start = ((), (), s32[]{:S(2)}) async-start(), calls=%async_computation.15 | async-start | bytes 3932160 | tf_op jit(solution)/shard_map/all_gather | solution.py:197
  224.4 143.6 %all-to-all-start = ((bf16[8,512,768]{2,1,0:T(8,128)(2,1)}), bf16[8,512,768]{2,1,0:T(8,128)(2,1)}, u32[]{:S(2)}, u32[]{:S(2)}) async-start(bf16[8,512,768]{2,1,0:T(8,128)(2,1)} %broadcast_select_fusion.1), calls=%async_computation | async-start | bytes 12582912 | tf_op jit(solution)/shard_map/all_to_all | solution.py:295
  391.0 141.9 %all-to-all-start.1 = ((bf16[8,512,768]{2,1,0:T(8,128)(2,1)}), bf16[8,512,768]{2,1,0:T(8,128)(2,1)}, u32[]{:S(2)}, u32[]{:S(2)}) async-start(bf16[8,512,768]{2,1,0:T(8,128)(2,1)} %convolution_convert_fusion), calls=%async_computation.1 | async-start | bytes 12582912 | tf_op jit(solution)/shard_map/all_to_all | solution.py:298
  396.0 189.0 %reduce-scatter.16.cloned.1.call-start = ((), (), s32[]{:S(2)}) async-start(), calls=%async_computation.21 | async-start | bytes 327680 | tf_op jit(solution)/shard_map/reduce_scatter | solution.py:203
  565.3 60.7 %all-gather.18.cloned.1.call-start = ((), (), s32[]{:S(2)}) async-start(), calls=%async_computation.18 | async-start | bytes 5898240 | tf_op jit(solution)/shard_map/all_gather | solution.py:197
  657.6 143.0 %copy-start.72 = (f32[1,512,768]{2,1,0:T(8,128)S(1)}, f32[1,512,768]{2,1,0:T(8,128)}, u32[]{:S(2)}) copy-start(f32[1,512,768]{2,1,0:T(8,128)} %param.55) | copy-start | bytes 4718596
  835.9 136.7 %copy-start.19 = (bf16[1024,2,768]{2,0,1:T(8,128)(2,1)S(1)}, bf16[1024,2,768]{2,0,1:T(8,128)(2,1)}, u32[]{:S(2)}) copy-start(bf16[1024,2,768]{2,0,1:T(8,128)(2,1)} %all-gather.14.cloned.1.call-done) | copy-start | bytes 9437188
  835.9 242.1 %all-to-all-start.3 = ((bf16[8,512,768]{2,1,0:T(8,128)(2,1)}), bf16[8,512,768]{2,1,0:T(8,128)(2,1)}, u32[]{:S(2)}, u32[]{:S(2)}) async-start(bf16[8,512,768]{2,1,0:T(8,128)(2,1)} %bitcast_convert_fusion), calls=%async_computation.4 | async-start | bytes 12582912 | tf_op jit(solution)/shard_map/all_to_all | solution.py:298
  841.0 131.7 %all-gather.16.cloned.1.call-start = ((), (), s32[]{:S(2)}) async-start(), calls=%async_computation.16 | async-start | bytes 1769472 | tf_op jit(solution)/shard_map/all_gather | solution.py:259
  841.8 200.6 %reduce-scatter.24.cloned.1.call-start = ((), (), s32[]{:S(2)}) async-start(), calls=%async_computation.25 | async-start | bytes 884736 | tf_op jit(solution)/shard_map/reduce_scatter | solution.py:404
  977.9 64.5 %copy-start.43 = (f32[512,96]{0,1:T(8,128)S(1)}, f32[512,96]{0,1:T(8,128)}, u32[]{:S(2)}) copy-start(f32[512,96]{0,1:T(8,128)} %param.50) | copy-start | bytes 589828
  981.5 191.9 %reduce-scatter.12.cloned.1.call-start = ((), (), s32[]{:S(2)}) async-start(), calls=%async_computation.19 | async-start | bytes 1966080 | tf_op jit(solution)/shard_map/reduce_scatter | solution.py:203
  1130.6 76.3 %reduce-scatter.10.cloned.1.call-start = ((), (), s32[]{:S(2)}) async-start(), calls=%async_computation.17 | async-start | bytes 1966080 | tf_op jit(solution)/shard_map/reduce_scatter | solution.py:203
  1173.2 113.3 %reduce-scatter.14.cloned.1.call-start = ((), (), s32[]{:S(2)}) async-start(), calls=%async_computation.20 | async-start | bytes 3932160 | tf_op jit(solution)/shard_map/reduce_scatter | solution.py:365
  1248.4 107.1 %reduce-scatter.22.cloned.1.call-start = ((), (), s32[]{:S(2)}) async-start(), calls=%async_computation.24 | async-start | bytes 1769472 | tf_op jit(solution)/shard_map/reduce_scatter | solution.py:401
  1254.2 204.2 %reduce-scatter.20.cloned.1.call-start = ((), (), s32[]{:S(2)}) async-start(), calls=%async_computation.23 | async-start | bytes 2433024 | tf_op jit(solution)/shard_map/reduce_scatter | solution.py:392
  1257.1 325.9 %reduce-scatter.18.cloned.1.call-start = ((), (), s32[]{:S(2)}) async-start(), calls=%async_computation.22 | async-start | bytes 7299072 | tf_op jit(solution)/shard_map/reduce_scatter | solution.py:391
  1388.1 70.2 %copy-start.37 = (f32[24,768]{1,0:T(8,128)S(1)}, f32[24,768]{1,0:T(8,128)}, u32[]{:S(2)}) copy-start(f32[24,768]{1,0:T(8,128)} %param.40) | copy-start | bytes 221188
  1388.1 70.2 %copy-start.52 = (f32[24,768]{1,0:T(8,128)S(1)}, f32[24,768]{1,0:T(8,128)}, u32[]{:S(2)}) copy-start(f32[24,768]{1,0:T(8,128)} %param.42) | copy-start | bytes 221188
  1388.2 70.2 %copy-start.53 = (f32[24,768]{1,0:T(8,128)S(1)}, f32[24,768]{1,0:T(8,128)}, u32[]{:S(2)}) copy-start(f32[24,768]{1,0:T(8,128)} %param.41) | copy-start | bytes 221188
  1460.0 123.0 %copy-start.27 = (f32[24,2304]{1,0:T(8,128)S(1)}, f32[24,2304]{1,0:T(8,128)}, u32[]{:S(2)}) copy-start(f32[24,2304]{1,0:T(8,128)} %param.37) | copy-start | bytes 663556
  (82 other events, 1383.5 us)
Sparse Core Ops, SparseCore 0:
  12.3 61.7 all-gather.7
  79.7 26.1 all-gather.9
  109.4 55.2 all-gather.11
  169.6 26.2 all-gather.13
  565.4 19.5 reduce-scatter.15
  588.1 37.7 all-gather.17
  1130.7 33.3 reduce-scatter.11
  1173.4 33.4 reduce-scatter.9
  1248.5 37.9 reduce-scatter.13
  1290.8 64.7 reduce-scatter.21
  1360.8 97.4 reduce-scatter.19
  1464.8 118.0 reduce-scatter.17
Sparse Core Ops, SparseCore 1:
  844.4 128.2 all-gather.15
  981.5 60.8 reduce-scatter.23
where the time goes:
time: 1610 us; the launch traced here: 1590 us
  waiting for transfers between devices  848 us (53%)
  blocking collectives  248 us (15%)
  local copies, waits for them, and re-layouts  170 us (11%)
  other arithmetic  150 us (9%)
  matrix products  139 us (9%)
  between operations  17.3 us (1%)
  starting transfers between devices  16.8 us (1%)
    all_to_all x1, blocking collectives, move_out(): lax.all_to_all(buffer, 'wide', split_axis=0, concat_axis=0, tiled=True)  143 us
    all_to_all x1, waiting for transfers between devices, move_out(): lax.all_to_all(buffer, 'wide', split_axis=0, concat_axis=0, tiled=True)  135 us
    all_gather x1, waiting for transfers between devices, body(): lax.all_gather(shared_in.astype(jnp.bfloat16), 'wide', axis=0, tiled=True)  131 us
    all_to_all x2, waiting for transfers between devices, move_back(): lax.all_to_all(buffer.astype(jnp.bfloat16), 'wide', split_axis=0, concat_...  121 us
    reduce_scatter x1, waiting for transfers between devices, body(): lax.psum_scatter(grad_mix_in, ('wide', 'tensor'), scatter_dimension=0, ti...  77 us
    reduce_scatter x1, waiting for transfers between devices, body(): lax.psum_scatter(grad_mix_out, ('wide', 'tensor'), scatter_dimension=0, t...  63.9 us
    reduce_scatter x1, waiting for transfers between devices, body(): lax.psum_scatter(grad_sh_out.astype(jnp.bfloat16), 'wide', scatter_dimens...  60.9 us
    reduce_scatter x1, waiting for transfers between devices, body(): lax.psum_scatter(grad_sh_in.astype(jnp.bfloat16), 'wide', scatter_dimensi...  60.7 us
  transfers between devices with their start and end apart: 17, of which 15 were waited for; matrix products, arithmetic and copies ran while one was open for 12% of the time, Pallas kernels for 0%

commit v1 on v0

v1 whole, which is shorter than its diff:
```python
import math

import jax
import jax.numpy as jnp
from jax import lax
from jax.sharding import PartitionSpec as P

HEAD = 64
TOP = 2
TRUNK = 256
SEG = 64
STEP = 5
SEGS = 13


NORM_EPS = 1e-06
BETA_ONE = 0.5
BETA_TWO = 0.5
ADAM_EPS = 1e-08
DECAY = 0.01
RATES = (0.02, 0.15, 0.3, 0.02, 0.012, 0.02, 0.012)

LOW = jnp.bfloat16
FULL = jnp.float32


def dot(a, b):
    return jnp.dot(a, b, preferred_element_type=FULL)


def dot_nt(a, b):
    return lax.dot_general(a, b, (((1,), (1,)), ((), ())), preferred_element_type=FULL)


def dot_tn(a, b):
    return lax.dot_general(a, b, (((0,), (0,)), ((), ())), preferred_element_type=FULL)


def rms_factor(values):
    return lax.rsqrt(jnp.mean(values * values, axis=-1, keepdims=True) + NORM_EPS)


def rms_back(values, factor, gain, grad):
    hat = values * factor
    scaled = grad * gain
    return factor * (scaled - hat * jnp.mean(scaled * hat, axis=-1, keepdims=True)), hat


def rotary_tables(position):
    half = HEAD // 2
    frequency = 10000.0 ** (-jnp.arange(half, dtype=FULL) / half)
    angles = position[:, None] * frequency[None, :]
    return jnp.cos(angles)[:, None, :], jnp.sin(angles)[:, None, :]


def rotate(values, cosine, sine):
    half = values.shape[-1] // 2
    one, two = values[..., :half], values[..., half:]
    return jnp.concatenate([one * cosine - two * sine, two * cosine + one * sine], axis=-1)


def tree_layout(parent_row, places):
    segment = jnp.where(places < TRUNK, 0, 1 + (places - TRUNK) // SEG)
    seg_start = jnp.where(segment == 0, 0, TRUNK + (segment - 1) * SEG)
    matches = segment[:, None] == jnp.arange(SEGS, dtype=jnp.int32)[None, :]
    upward = jnp.sum(jnp.where(matches, parent_row[None, :], 0), axis=1)
    depth_base = jnp.where(upward == 0, TRUNK, TRUNK + SEG)
    position = jnp.where(segment == 0, places, depth_base + places - seg_start)
    return (segment, upward, position)


def allowed_mask(segment, upward, places):
    same_segment = (segment[None, :] == segment[:, None]) & (places[None, :] <= places[:, None])
    ancestor = (segment[:, None] != 0) & (
        (segment[None, :] == 0) | (segment[None, :] == upward[:, None])
    )
    return same_segment | ancestor


def attend_forward(queries, keys, values, allowed):
    scale = 1.0 / math.sqrt(HEAD)
    scores = jnp.einsum("qhd,khd->hqk", queries, keys, preferred_element_type=FULL) * scale
    scores = jnp.where(allowed[None], scores, -1e30)
    row_top = jnp.max(scores, axis=-1, keepdims=True)
    shifted = jnp.exp(scores - row_top)
    row_total = jnp.sum(shifted, axis=-1, keepdims=True)
    weights = (shifted / row_total).astype(LOW)
    attended = jnp.einsum("hqk,khd->qhd", weights, values, preferred_element_type=FULL)
    return attended, row_top + jnp.log(row_total)


def attend_backward(queries, keys, values, allowed, grad_attended, log_totals):
    scale = 1.0 / math.sqrt(HEAD)
    scores = jnp.einsum("qhd,khd->hqk", queries, keys, preferred_element_type=FULL) * scale
    scores = jnp.where(allowed[None], scores, -1e30)
    probs = jnp.exp(scores - log_totals)
    grad_probs = jnp.einsum("qhd,khd->hqk", grad_attended, values, preferred_element_type=FULL)
    inner = jnp.sum(probs * grad_probs, axis=-1, keepdims=True)
    grad_scores = (probs * (grad_probs - inner)).astype(LOW)
    grad_query = jnp.einsum("hqk,khd->qhd", grad_scores, keys, preferred_element_type=FULL) * scale
    grad_key = jnp.einsum("hqk,qhd->khd", grad_scores, queries, preferred_element_type=FULL) * scale
    grad_value = jnp.einsum(
        "hqk,qhd->khd", probs.astype(LOW), grad_attended, preferred_element_type=FULL
    )
    return grad_query, grad_key, grad_value


def branch_forward(rows, w_gate, w_up):
    gate, up = dot(rows, w_gate), dot(rows, w_up)
    return gate, up, (jax.nn.silu(gate) * up).astype(LOW)


def branch_activation_grads(gate, up, grad_hidden):
    sigmoid = jax.nn.sigmoid(gate)
    grad_gate = grad_hidden * up * sigmoid * (1.0 + gate * (1.0 - sigmoid))
    grad_up = grad_hidden * gate * sigmoid
    return grad_gate.astype(LOW), grad_up.astype(LOW)


def adam_step(weight, mean_old, square_old, gradient, rate):
    mean_new = BETA_ONE * mean_old + (1.0 - BETA_ONE) * gradient
    square_new = BETA_TWO * square_old + (1.0 - BETA_TWO) * gradient * gradient
    mean_hat = mean_new / (1.0 - BETA_ONE**STEP)
    square_hat = square_new / (1.0 - BETA_TWO**STEP)
    updated = weight - rate * (mean_hat / (jnp.sqrt(square_hat) + ADAM_EPS) + DECAY * weight)
    return (mean_new, square_new, updated)


def swap_with(value, mask, count):
    return lax.ppermute(value, "tensor", [(i, i ^ mask) for i in range(count)])


def gather_chunks(parts, count):
    if count != 4:
        whole = [lax.all_gather(p, "tensor", axis=0) for p in parts]
        return [[w[j] for w in whole] for j in range(count)]
    far = [swap_with(p, 2, count) for p in parts]
    near = [swap_with(p, 1, count) for p in parts]
    both = [swap_with(p, 1, count) for p in far]
    return [parts, near, far, both]


def scatter_chunks(chunks, count):
    parts = range(len(chunks[0]))
    if count != 4:
        sums = []
        for p in parts:
            stacked = jnp.stack([chunks[j][p].astype(LOW) for j in range(count)])
            got = lax.all_to_all(stacked, "tensor", split_axis=0, concat_axis=0, tiled=True)
            sums.append(jnp.sum(got.astype(FULL), axis=0))
        return sums
    far = [swap_with(chunks[3][p].astype(LOW), 1, count) for p in parts]
    near = [swap_with(chunks[1][p].astype(LOW), 1, count) for p in parts]
    across = [
        swap_with((chunks[2][p] + far[p].astype(FULL)).astype(LOW), 2, count) for p in parts
    ]
    return [chunks[0][p] + near[p].astype(FULL) + across[p].astype(FULL) for p in parts]


def sum_rows(terms):
    return lax.psum_scatter(
        terms.astype(LOW), "tensor", scatter_dimension=0, tiled=True
    ).astype(FULL)


def exchange(value):
    return lax.all_to_all(value, "wide", split_axis=0, concat_axis=0, tiled=True)


def body(
    tokens,
    cotangent,
    gate_logits,
    routes,
    parents,
    mixing_in,
    mixing_in_mean,
    mixing_in_square,
    mixing_out,
    mixing_out_mean,
    mixing_out_square,
    norm_gains,
    norm_gains_mean,
    norm_gains_square,
    shared_in,
    shared_in_mean,
    shared_in_square,
    shared_out,
    shared_out_mean,
    shared_out_square,
    expert_in,
    expert_in_mean,
    expert_in_square,
    expert_out,
    expert_out_mean,
    expert_out_square,
):
    rows_dev, width = tokens.shape
    wide = lax.axis_size("wide")
    count = lax.axis_size("tensor")
    rank = lax.axis_index("tensor")
    tree_length = rows_dev * count
    capacity = 2 * rows_dev * TOP // wide
    slots = wide * capacity
    heads = width // HEAD
    heads_dev = -(-heads // count)
    head_pad = heads_dev * count - heads
    head_width = heads_dev * HEAD
    rows_weight = mixing_in.shape[0]

    cut = mixing_in.astype(LOW).reshape(rows_weight, 3, heads, HEAD)
    cut = jnp.pad(cut, ((0, 0), (0, 0), (0, head_pad), (0, 0)))
    cut = cut.reshape(rows_weight, 3, count, head_width).transpose(2, 0, 1, 3)
    cut = cut.reshape(count, rows_weight, 3 * head_width)
    gain_columns = jnp.broadcast_to(norm_gains.astype(LOW).T[None], (count, rows_weight, 2))
    cut = jnp.concatenate([cut, gain_columns], axis=2)
    sent = jnp.broadcast_to(cut[None], (wide,) + cut.shape).reshape(
        wide * count, rows_weight, 3 * head_width + 2
    )
    got = lax.all_to_all(sent, ("wide", "tensor"), split_axis=0, concat_axis=0, tiled=True)
    got = got.reshape(width, 3 * head_width + 2)
    w_qkv = got[:, : 3 * head_width]
    gain_pair = got[:, 3 * head_width :].astype(FULL).T

    tokens_all = lax.all_gather(tokens, "tensor", axis=0, tiled=True)
    w_mix_out = lax.all_gather(
        mixing_out.astype(LOW), ("wide", "tensor"), axis=0, tiled=True
    )
    shared_low = jnp.concatenate(
        [shared_in.astype(LOW), shared_out.astype(LOW).T[:, None]], axis=1
    )
    w_shared = lax.all_gather(shared_low, "wide", axis=0, tiled=True)
    cotangent_all = lax.all_gather(cotangent, "tensor", axis=0, tiled=True)
    expert_chunks = gather_chunks(
        [
            expert_in[0, :, 0].astype(LOW),
            expert_in[0, :, 1].astype(LOW),
            expert_out[0].astype(LOW),
        ],
        count,
    )

    own_routes = lax.dynamic_slice_in_dim(routes, rank * rows_dev, rows_dev, 0)
    own_logits = lax.dynamic_slice_in_dim(gate_logits, rank * rows_dev, rows_dev, 0)
    gates = jax.nn.softmax(own_logits, axis=-1)
    flat = own_routes.reshape(-1)
    named = (flat[:, None] == jnp.arange(wide, dtype=jnp.int32)[None, :]).astype(LOW)
    order = jnp.arange(flat.shape[0], dtype=jnp.int32)
    earlier = (order[None, :] < order[:, None]).astype(LOW)
    before = jnp.sum(dot(earlier, named) * named.astype(FULL), axis=1).astype(jnp.int32)
    places = (flat * capacity + before).reshape(rows_dev, TOP)
    slot_ids = jnp.arange(slots, dtype=jnp.int32)
    picks = [(slot_ids[:, None] == places[:, k][None, :]).astype(LOW) for k in range(TOP)]
    pick_any = picks[0] + picks[1]
    grad_out = cotangent.astype(FULL)
    grad_routes = [(gates[:, k : k + 1] * grad_out).astype(LOW) for k in range(TOP)]
    grad_slots = (dot(picks[0], grad_routes[0]) + dot(picks[1], grad_routes[1])).astype(LOW)
    expert_grads = exchange(grad_slots.reshape(wide, capacity, width)).reshape(slots, width)

    tree_places = jnp.arange(tree_length, dtype=jnp.int32)
    segment, upward, position = tree_layout(parents[0], tree_places)
    allowed = allowed_mask(segment, upward, tree_places)
    cosine, sine = rotary_tables(position.astype(FULL))
    tree_rows = tokens_all.astype(FULL)
    normed_one = (tree_rows * rms_factor(tree_rows) * gain_pair[0]).astype(LOW)
    projected = dot(normed_one, w_qkv).reshape(tree_length, 3, heads_dev, HEAD)
    queries = rotate(projected[:, 0], cosine, sine).astype(LOW)
    keys = rotate(projected[:, 1], cosine, sine).astype(LOW)
    values = projected[:, 2].astype(LOW)
    attended, log_totals = attend_forward(queries, keys, values, allowed)
    attended_low = lax.all_to_all(
        attended.astype(LOW).reshape(tree_length, head_width),
        "tensor",
        split_axis=0,
        concat_axis=1,
        tiled=True,
    )[:, :width]
    input_rows = tokens.astype(FULL)
    residual = input_rows + dot(attended_low, w_mix_out)
    factor_two = rms_factor(residual)
    normed_two = (residual * factor_two * gain_pair[1]).astype(LOW)

    row_slots = dot(pick_any, normed_two).astype(LOW)
    expert_rows = exchange(row_slots.reshape(wide, capacity, width)).reshape(slots, width)
    shared_rows = lax.all_gather(normed_two, "tensor", axis=0, tiled=True)
    sh_gate_w, sh_up_w, sh_out_t = w_shared[:, 0], w_shared[:, 1], w_shared[:, 2]
    sh_gate, sh_up, sh_hidden = branch_forward(shared_rows, sh_gate_w, sh_up_w)
    sh_grad_hidden = dot(cotangent_all, sh_out_t)
    sh_ggate, sh_gup = branch_activation_grads(sh_gate, sh_up, sh_grad_hidden)
    sh_grad_rows = sum_rows(dot_nt(sh_ggate, sh_gate_w) + dot_nt(sh_gup, sh_up_w))
    sh_part = sum_rows(dot_nt(sh_hidden, sh_out_t))
    sh_grads = jnp.stack(
        [
            dot_tn(shared_rows, sh_ggate).astype(LOW),
            dot_tn(shared_rows, sh_gup).astype(LOW),
            dot_tn(cotangent_all, sh_hidden).astype(LOW),
        ],
        axis=1,
    )

    states = []
    grad_rows = 0.0
    for gate_w, up_w, out_w in expert_chunks:
        gate, up, hidden = branch_forward(expert_rows, gate_w, up_w)
        ggate, gup = branch_activation_grads(gate, up, dot_nt(expert_grads, out_w))
        grad_rows = grad_rows + dot_nt(ggate, gate_w) + dot_nt(gup, up_w)
        states.append((hidden, ggate, gup))
    back_rows = exchange(grad_rows.astype(LOW).reshape(wide, capacity, width))
    back_rows = back_rows.reshape(slots, width)
    out_rows = 0.0
    for (hidden, _, _), (_, _, out_w) in zip(states, expert_chunks):
        out_rows = out_rows + dot(hidden, out_w)
    returned = exchange(out_rows.astype(LOW).reshape(wide, capacity, width))
    returned = returned.reshape(slots, width)
    weight_grads = [
        [dot_tn(expert_rows, ggate), dot_tn(expert_rows, gup), dot_tn(hidden, expert_grads)]
        for hidden, ggate, gup in states
    ]
    grad_ex_gate, grad_ex_up, grad_ex_out = scatter_chunks(weight_grads, count)
    grad_ex_in = jnp.stack([grad_ex_gate, grad_ex_up], axis=1)

    grad_normed_two = dot_tn(pick_any, back_rows) + sh_grad_rows
    grad_part, hat_two = rms_back(residual, factor_two, gain_pair[1], grad_normed_two)
    gain_two_part = jnp.sum(grad_normed_two * hat_two, axis=0)
    grad_residual = grad_out + grad_part
    grad_res_low = grad_residual.astype(LOW)
    grad_attended = dot_nt(grad_res_low, w_mix_out).astype(LOW)
    grad_attended = jnp.pad(grad_attended, ((0, 0), (0, head_pad * HEAD)))
    grad_attended = lax.all_to_all(
        grad_attended, "tensor", split_axis=1, concat_axis=0, tiled=True
    ).reshape(tree_length, heads_dev, HEAD)
    grad_mix_out = dot_tn(attended_low, grad_res_low).astype(LOW)
    grad_mix_out = lax.all_to_all(
        grad_mix_out.reshape(wide * count, rows_weight, width),
        ("wide", "tensor"),
        split_axis=0,
        concat_axis=0,
        tiled=True,
    )
    grad_mix_out = jnp.sum(grad_mix_out.astype(FULL), axis=0)

    grad_query, grad_key, grad_value = attend_backward(
        queries, keys, values, allowed, grad_attended, log_totals
    )
    grad_projected = jnp.stack(
        [rotate(grad_query, cosine, -sine), rotate(grad_key, cosine, -sine), grad_value], axis=1
    )
    grad_projected = grad_projected.astype(LOW).reshape(tree_length, 3 * head_width)
    grad_normed_one = sum_rows(dot_nt(grad_projected, w_qkv))
    grad_mix_in = dot_tn(normed_one, grad_projected).astype(LOW)
    sent = jnp.concatenate([grad_mix_in, gain_two_part.astype(LOW)[:, None]], axis=1)
    got = lax.all_to_all(
        sent.reshape(wide * count, rows_weight, 3 * head_width + 1),
        ("wide", "tensor"),
        split_axis=0,
        concat_axis=0,
        tiled=True,
    )
    got = jnp.sum(got.astype(FULL).reshape(wide, count, rows_weight, -1), axis=0)
    grad_gain_two = jnp.sum(got[:, :, 3 * head_width], axis=0)
    grad_mix_in = got[:, :, : 3 * head_width].reshape(count, rows_weight, 3, head_width)
    grad_mix_in = grad_mix_in.transpose(1, 2, 0, 3).reshape(rows_weight, 3, count * head_width)
    grad_mix_in = grad_mix_in[:, :, :width].reshape(rows_weight, 3 * width)
    grad_gain_one = jnp.sum(mixing_in.astype(LOW).astype(FULL) * grad_mix_in, axis=1)
    grad_gain_one = grad_gain_one / norm_gains[0].astype(LOW).astype(FULL)

    grad_part, _ = rms_back(input_rows, rms_factor(input_rows), gain_pair[0], grad_normed_one)
    input_grad = grad_residual + grad_part

    per_route = [dot_tn(picks[k], returned) for k in range(TOP)]
    mixed = (
        residual + gates[:, :1] * per_route[0] + gates[:, 1:] * per_route[1] + sh_part
    )
    gate_grad = jnp.stack([jnp.sum(grad_out * rows, axis=-1) for rows in per_route], axis=1)
    logit_grad = gates * (gate_grad - jnp.sum(gates * gate_grad, axis=-1, keepdims=True))

    sh_grads = exchange(sh_grads.reshape(wide, width // wide, 3, -1))
    sh_grads = jnp.sum(sh_grads.astype(FULL), axis=0)

    weights = (mixing_in, mixing_out, norm_gains, shared_in, shared_out, expert_in, expert_out)
    means = (
        mixing_in_mean,
        mixing_out_mean,
        norm_gains_mean,
        shared_in_mean,
        shared_out_mean,
        expert_in_mean,
        expert_out_mean,
    )
    squares = (
        mixing_in_square,
        mixing_out_square,
        norm_gains_square,
        shared_in_square,
        shared_out_square,
        expert_in_square,
        expert_out_square,
    )
    gradients = (
        grad_mix_in,
        grad_mix_out,
        jnp.stack([grad_gain_one, grad_gain_two]),
        sh_grads[:, :2],
        sh_grads[:, 2].T,
        grad_ex_in[None],
        grad_ex_out[None],
    )
    results = [mixed.astype(LOW), input_grad, logit_grad]
    for number in range(7):
        results.extend(
            adam_step(
                weights[number], means[number], squares[number], gradients[number], RATES[number]
            )
        )
    return tuple(results)


def solution(mesh):
    placed = (
        P(("wide", "tensor"), None),
        P(("wide", "tensor"), None),
        P("wide", None),
        P("wide", None),
        P("wide", None),
        P(("wide", "tensor"), None),
        P(("wide", "tensor"), None),
        P(("wide", "tensor"), None),
        P(("wide", "tensor"), None),
        P(("wide", "tensor"), None),
        P(("wide", "tensor"), None),
        P(None, ("wide", "tensor")),
        P(None, ("wide", "tensor")),
        P(None, ("wide", "tensor")),
        P("wide", None, "tensor"),
        P("wide", None, "tensor"),
        P("wide", None, "tensor"),
        P("tensor", "wide"),
        P("tensor", "wide"),
        P("tensor", "wide"),
        P("wide", None, None, "tensor"),
        P("wide", None, None, "tensor"),
        P("wide", None, None, "tensor"),
        P("wide", "tensor", None),
        P("wide", "tensor", None),
        P("wide", "tensor", None),
    )
    return jax.shard_map(
        body,
        mesh=mesh,
        in_specs=placed,
        out_specs=(
            P(("wide", "tensor"), None),
            P(("wide", "tensor"), None),
            P(("wide", "tensor"), None),
            P(("wide", "tensor"), None),
            P(("wide", "tensor"), None),
            P(("wide", "tensor"), None),
            P(("wide", "tensor"), None),
            P(("wide", "tensor"), None),
            P(("wide", "tensor"), None),
            P(None, ("wide", "tensor")),
            P(None, ("wide", "tensor")),
            P(None, ("wide", "tensor")),
            P("wide", None, "tensor"),
            P("wide", None, "tensor"),
            P("wide", None, "tensor"),
            P("tensor", "wide"),
            P("tensor", "wide"),
            P("tensor", "wide"),
            P("wide", None, None, "tensor"),
            P("wide", None, None, "tensor"),
            P("wide", None, None, "tensor"),
            P("wide", "tensor", None),
            P("wide", "tensor", None),
            P("wide", "tensor", None),
        ),
        check_vma=False,
    )
```

time: 1610 us -> 559 us (0.35)
  the two profiles are of different devices: /device:TPU:3 before, /device:TPU:0 now
where the time goes in v1:
time: 559 us; the launch traced here: 548 us
  waiting for transfers between devices  205 us (37%)
  matrix products  177 us (32%)
  starting transfers between devices  58.1 us (10%)
  other arithmetic  54.4 us (10%)
  local copies, waits for them, and re-layouts  37.8 us (7%)
  between operations  16.5 us (3%)
    all_to_all x5, waiting for transfers between devices, exchange(): lax.all_to_all(value, 'wide', split_axis=0, concat_axis=0, tiled=True)  129 us
    dot_general x21, matrix products, dot(): return jnp.dot(a, b, preferred_element_type=FULL)  57.4 us
    dot_general x20, matrix products, dot_tn(): lax.dot_general(a, b, (((0,), (0,)), ((), ())), preferred_element_type=FULL)  55.6 us
    dot_general x17, matrix products, dot_nt(): lax.dot_general(a, b, (((1,), (1,)), ((), ())), preferred_element_type=FULL)  44.3 us
    all_gather x1, waiting for transfers between devices, body(): lax.all_gather(mixing_out.astype(LOW), ('wide', 'tensor'), axis=0, tiled=...  33.8 us
    unnamed x261, local copies, waits for them, and re-layouts  26.5 us
    all_to_all x5, starting transfers between devices, exchange(): lax.all_to_all(value, 'wide', split_axis=0, concat_axis=0, tiled=True)  22.4 us
    all_to_all x1, waiting for transfers between devices, body(): lax.all_to_all(sent, ('wide', 'tensor'), split_axis=0, concat_axis=0, til...  19.9 us
  transfers between devices with their start and end apart: 36, of which 11 were waited for; matrix products, arithmetic and copies ran while one was open for 46% of the time, Pallas kernels for 0%

profile of v1, /device:TPU:0, one launch (start us, length us, event | category | flops | bytes accessed | tf_op | source)
XLA Modules:
  0.0 548.4 jit_solution(12999505524465037670)
XLA Ops:
  12.9 7.3 %all-to-all-start = ((bf16[32,24,578]{2,1,0:T(8,128)(2,1)}), bf16[32,24,578]{2,1,0:T(8,128)(2,1)S(1)}, u32[]{:S(2)}, u32[]{:S(2)}) async-start(bf16[32,24,578]{2,1,0:T(8,128)(2,1)} %bitcast.2), calls=%async_computation | async-start | bytes 1966080 | tf_op jit(solution)/shard_map/all_to_all | solution.py:220
  25.2 19.9 %all-to-all-done = bf16[32,24,578]{2,1,0:T(8,128)(2,1)S(1)} async-done(((bf16[32,24,578]{2,1,0:T(8,128)(2,1)}), bf16[32,24,578]{2,1,0:T(8,128)(2,1)S(1)}, u32[]{:S(2)}, u32[]{:S(2)}) %all-to-all-start) | async-done | bytes 887840 | tf_op jit(solution)/shard_map/all_to_all | solution.py:220
  65.4 33.8 %all-gather.8.cloned.1.call-done = bf16[768,768]{1,0:T(8,128)(2,1)} async-done(((bf16[24,768]{1,0:T(8,128)(2,1)}), bf16[768,768]{1,0:T(8,128)(2,1)}) %all-gather.8.cloned.1.call-update) | async-done | bytes 1179664 | tf_op jit(solution)/shard_map/all_gather | solution.py:226
  104.7 4.7 all-to-all-start.2
  113.7 42.9 %all-to-all-done.2 = bf16[8,128,768]{2,1,0:T(8,128)(2,1)} async-done(((bf16[8,128,768]{2,1,0:T(8,128)(2,1)}), bf16[8,128,768]{2,1,0:T(8,128)(2,1)}, u32[]{:S(2)}, u32[]{:S(2)}) %all-to-all-start.2) | async-done | bytes 1572896 | tf_op jit(solution)/shard_map/all_to_all | solution.py:167
  162.9 4.6 multiply_convert_fusion.13
  168.1 9.9 %collective-permute-done.5 = bf16[512,768]{1,0:T(8,128)(2,1)S(1)} collective-permute-done((bf16[512,768]{1,0:T(8,128)(2,1)}, bf16[512,768]{1,0:T(8,128)(2,1)S(1)}, u32[]{:S(2)}, u32[]{:S(2)}) %collective-permute-start.5) | collective-permute-done | bytes 786464 | tf_op jit(solution)/shard_map/ppermute | solution.py:130
  180.9 4.9 multiply_convert_fusion.11
  185.8 4.5 multiply_convert_fusion.12
  198.8 4.9 multiply_convert_fusion.10
  205.9 4.7 all-to-all-start.3
  217.4 4.5 fusion.16
  233.0 15.0 %all-to-all-done.3 = bf16[8,128,768]{2,1,0:T(8,128)(2,1)S(1)} async-done(((bf16[8,128,768]{2,1,0:T(8,128)(2,1)}), bf16[8,128,768]{2,1,0:T(8,128)(2,1)S(1)}, u32[]{:S(2)}, u32[]{:S(2)}) %all-to-all-start.3) | async-done | bytes 1572896 | tf_op jit(solution)/shard_map/all_to_all | solution.py:167
  248.0 4.4 all-to-all-start.9
  263.5 42.3 %all-to-all-done.9 = bf16[8,96,3,512]{3,1,2,0:T(8,128)(2,1)} async-done(((bf16[8,96,3,512]{3,1,2,0:T(8,128)(2,1)}), bf16[8,96,3,512]{3,1,2,0:T(8,128)(2,1)}, u32[]{:S(2)}, u32[]{:S(2)}) %all-to-all-start.9) | async-done | bytes 2359328 | tf_op jit(solution)/shard_map/all_to_all | solution.py:167
  321.0 25.7 %all-to-all-done.4 = bf16[8,128,768]{2,1,0:T(8,128)(2,1)} async-done(((bf16[8,128,768]{2,1,0:T(8,128)(2,1)}), bf16[8,128,768]{2,1,0:T(8,128)(2,1)}, u32[]{:S(2)}, u32[]{:S(2)}) %all-to-all-start.4) | async-done | bytes 1572896 | tf_op jit(solution)/shard_map/all_to_all | solution.py:167
  346.7 4.7 multiply_convert_fusion.7
  442.9 6.2 %multiply_reduce_fusion = (f32[3,1024]{1,0:T(4,128)S(1)}, f32[3,1024,1024]{1,2,0:T(8,128)S(1)}) fusion(f32[3,1024,1024]{1,2,0:T(8,128)} %copy-done.2, f32[3,1024]{1,0:T(4,128)S(1)} %log_add_fusion, bf16[1024,3,64]{0,2,1:T(8,128)(2,1)S(1)} %reshape.536, f32[1024,3,3,64]{0,3,2,1:T(8,128)} %bitcast.242), kind=kOutput, calls=%fused_computation.1 | convolution fusion | flops 412087296 | bytes 25976832 | tf_op jit(solution)/shard_map/qhd,khd->hqk/dot_general | solution.py:97
  449.2 9.3 %multiply_convert_fusion = bf16[3,1024,1024]{1,2,0:T(8,128)(2,1)} fusion(f32[3,1024,1024]{1,2,0:T(8,128)S(1)} %get-tuple-element.225, f32[3,1024,1024]{1,2,0:T(8,128)} %copy-done.2, f32[3,1024]{1,0:T(4,128)S(1)} %get-tuple-element.224, f32[3,1024]{1,0:T(4,128)S(1)} %log_add_fusion), kind=kLoop, calls=%fused_computation | loop fusion | flops 12582912 | bytes 31481856 | tf_op jit(solution)/shard_map/convert_element_type | solution.py:99
  458.5 5.0 fusion.20
  472.0 5.9 %all-to-all-start.7 = ((bf16[32,24,577]{2,1,0:T(8,128)(2,1)}), bf16[32,24,577]{2,1,0:T(8,128)(2,1)}, u32[]{:S(2)}, u32[]{:S(2)}) async-start(bf16[32,24,577]{2,1,0:T(8,128)(2,1)} %pad_maximum_fusion.3), calls=%async_computation.10 | async-start | bytes 1966080 | tf_op jit(solution)/shard_map/all_to_all | solution.py:352
  496.3 6.4 %all-to-all-done.7 = bf16[32,24,577]{2,1,0:T(8,128)(2,1)} async-done(((bf16[32,24,577]{2,1,0:T(8,128)(2,1)}), bf16[32,24,577]{2,1,0:T(8,128)(2,1)}, u32[]{:S(2)}, u32[]{:S(2)}) %all-to-all-start.7) | async-done | bytes 886304 | tf_op jit(solution)/shard_map/all_to_all | solution.py:352
  506.5 6.7 %multiply_subtract_fusion = (f32[1,768,2,512]{3,1,2,0:T(8,128)S(1)}, f32[1,768,2,512]{3,1,2,0:T(8,128)S(1)}, f32[1,768,2,512]{3,1,2,0:T(8,128)S(1)}) fusion(f32[1,768,2,512]{3,2,1,0:T(2,128)} %param.46, f32[1,768,1,512]{3,1,2,0:T(8,128)} %add_bitcast_fusion, f32[1,768,1,512]{3,1,2,0:T(8,128)S(1)} %add_bitcast_fusion.1, f32[1,768,2,512]{3,2,1,0:T(2,128)} %param.48, ...), kind=kLoop, calls=%fused_computation.26 | loop fusion | flops 11796480 | bytes 22020096 | tf_op jit(solution)/shard_map/sub | solution.py:125
  525.5 4.5 multiply_subtract_fusion.1
  (465 shorter events, 249.2 us)
Async XLA Ops:
  8.0 91.2 %all-gather.8.cloned.1.call-start = ((), (), s32[]{:S(2)}) async-start(), calls=%async_computation.14 | async-start | bytes 1216512 | tf_op jit(solution)/shard_map/all_gather | solution.py:226
  9.5 201.1 %all-gather.14.cloned.1.call-start = ((), (), s32[]{:S(2)}) async-start(), calls=%async_computation.18 | async-start | bytes 1966080 | tf_op jit(solution)/shard_map/all_gather | solution.py:233
  20.2 190.4 %all-gather.12.cloned.1.call-start = ((), (), s32[]{:S(2)}) async-start(), calls=%async_computation.16 | async-start | bytes 2654208 | tf_op jit(solution)/shard_map/all_gather | solution.py:232
  104.7 51.9 %all-to-all-start.2 = ((bf16[8,128,768]{2,1,0:T(8,128)(2,1)}), bf16[8,128,768]{2,1,0:T(8,128)(2,1)}, u32[]{:S(2)}, u32[]{:S(2)}) async-start(bf16[8,128,768]{2,1,0:T(8,128)(2,1)} %bitcast.243), calls=%async_computation.2 | async-start | bytes 3145728 | tf_op jit(solution)/shard_map/all_to_all | solution.py:167
  109.4 105.1 %all-gather.10.cloned.1.call-start = ((), (), s32[]{:S(2)}) async-start(), calls=%async_computation.15 | async-start | bytes 1966080 | tf_op jit(solution)/shard_map/all_gather | solution.py:285
  110.1 48.9 %collective-permute-start.3 = (bf16[768,512]{1,0:T(8,128)(2,1)S(1)}, bf16[768,512]{1,0:T(8,128)(2,1)S(1)}, u32[]{:S(2)}, u32[]{:S(2)}) collective-permute-start(bf16[768,512]{1,0:T(8,128)(2,1)S(1)} %get-tuple-element.188), channel_id=1, source_target_pairs={{0,2},{1,3},{2,0},{3,1},{4,6},{5,7},{6,4},{7,5},{8,10},{9,11},{10,... | collective-permute-start | bytes 2359304 | tf_op jit(solution)/shard_map/ppermute | solution.py:130
  111.5 56.0 %collective-permute-start = (bf16[768,512]{1,0:T(8,128)(2,1)S(1)}, bf16[768,512]{1,0:T(8,128)(2,1)}, u32[]{:S(2)}, u32[]{:S(2)}) collective-permute-start(bf16[768,512]{1,0:T(8,128)(2,1)S(1)} %get-tuple-element.188), channel_id=1, source_target_pairs={{0,1},{1,0},{2,3},{3,2},{4,5},{5,4},{6,7},{7,6},{8,9},{9,8},{10,11... | collective-permute-start | bytes 2359304 | tf_op jit(solution)/shard_map/ppermute | solution.py:130
  111.5 74.3 %collective-permute-start.1 = (bf16[768,512]{1,0:T(8,128)(2,1)S(1)}, bf16[768,512]{1,0:T(8,128)(2,1)}, u32[]{:S(2)}, u32[]{:S(2)}) collective-permute-start(bf16[768,512]{1,0:T(8,128)(2,1)S(1)} %get-tuple-element.189), channel_id=1, source_target_pairs={{0,1},{1,0},{2,3},{3,2},{4,5},{5,4},{6,7},{7,6},{8,9},{9,8},{10,11... | collective-permute-start | bytes 2359304 | tf_op jit(solution)/shard_map/ppermute | solution.py:130
  112.0 55.6 %collective-permute-start.4 = (bf16[768,512]{1,0:T(8,128)(2,1)S(1)}, bf16[768,512]{1,0:T(8,128)(2,1)}, u32[]{:S(2)}, u32[]{:S(2)}) collective-permute-start(bf16[768,512]{1,0:T(8,128)(2,1)S(1)} %get-tuple-element.189), channel_id=1, source_target_pairs={{0,2},{1,3},{2,0},{3,1},{4,6},{5,7},{6,4},{7,5},{8,10},{9,11},{10,... | collective-permute-start | bytes 2359304 | tf_op jit(solution)/shard_map/ppermute | solution.py:130
  113.7 80.3 %collective-permute-start.2 = (bf16[512,768]{1,0:T(8,128)(2,1)}, bf16[512,768]{1,0:T(8,128)(2,1)}, u32[]{:S(2)}, u32[]{:S(2)}) collective-permute-start(bf16[512,768]{1,0:T(8,128)(2,1)} %convert_bitcast_fusion), channel_id=1, source_target_pairs={{0,1},{1,0},{2,3},{3,2},{4,5},{5,4},{6,7},{7,6},{8,9},{9,8},{10,11... | collective-permute-start | bytes 2359304 | tf_op jit(solution)/shard_map/ppermute | solution.py:130
  205.9 42.1 %all-to-all-start.3 = ((bf16[8,128,768]{2,1,0:T(8,128)(2,1)}), bf16[8,128,768]{2,1,0:T(8,128)(2,1)S(1)}, u32[]{:S(2)}, u32[]{:S(2)}) async-start(bf16[8,128,768]{2,1,0:T(8,128)(2,1)} %bitcast.234), calls=%async_computation.3 | async-start | bytes 3145728 | tf_op jit(solution)/shard_map/all_to_all | solution.py:167
  248.0 57.8 %all-to-all-start.9 = ((bf16[8,96,3,512]{3,1,2,0:T(8,128)(2,1)}), bf16[8,96,3,512]{3,1,2,0:T(8,128)(2,1)}, u32[]{:S(2)}, u32[]{:S(2)}) async-start(bf16[8,96,3,512]{3,1,2,0:T(8,128)(2,1)} %copy.189), calls=%async_computation.12 | async-start | bytes 4718592 | tf_op jit(solution)/shard_map/all_to_all | solution.py:167
  252.3 166.6 %reduce-scatter.6.cloned.1.call-start = ((), (), s32[]{:S(2)}) async-start(), calls=%async_computation.19 | async-start | bytes 1966080 | tf_op jit(solution)/shard_map/reduce_scatter | solution.py:161
  305.8 40.9 %all-to-all-start.4 = ((bf16[8,128,768]{2,1,0:T(8,128)(2,1)}), bf16[8,128,768]{2,1,0:T(8,128)(2,1)}, u32[]{:S(2)}, u32[]{:S(2)}) async-start(bf16[8,128,768]{2,1,0:T(8,128)(2,1)} %bitcast.27), calls=%async_computation.5 | async-start | bytes 3145728 | tf_op jit(solution)/shard_map/all_to_all | solution.py:167
  310.1 115.4 %reduce-scatter.4.cloned.1.call-start = ((), (), s32[]{:S(2)}) async-start(), calls=%async_computation.17 | async-start | bytes 1966080 | tf_op jit(solution)/shard_map/reduce_scatter | solution.py:161
  381.4 40.9 %all-to-all-start.5 = ((bf16[8,128,768]{2,1,0:T(8,128)(2,1)}), bf16[8,128,768]{2,1,0:T(8,128)(2,1)}, u32[]{:S(2)}, u32[]{:S(2)}) async-start(bf16[8,128,768]{2,1,0:T(8,128)(2,1)} %bitcast.29), calls=%async_computation.6 | async-start | bytes 3145728 | tf_op jit(solution)/shard_map/all_to_all | solution.py:167
  405.9 75.8 %collective-permute-start.16 = (bf16[512,768]{1,0:T(8,128)(2,1)}, bf16[512,768]{1,0:T(8,128)(2,1)}, u32[]{:S(2)}, u32[]{:S(2)}) collective-permute-start(bf16[512,768]{1,0:T(8,128)(2,1)} %convolution_convert_fusion.5), channel_id=1, source_target_pairs={{0,1},{1,0},{2,3},{3,2},{4,5},{5,4},{6,7},{7,6},{8,9},{9,8},{10,11... | collective-permute-start | bytes 2359304 | tf_op jit(solution)/shard_map/ppermute | solution.py:130
  406.3 79.3 %collective-permute-start.9 = (bf16[768,512]{1,0:T(8,128)(2,1)}, bf16[768,512]{1,0:T(8,128)(2,1)}, u32[]{:S(2)}, u32[]{:S(2)}) collective-permute-start(bf16[768,512]{1,0:T(8,128)(2,1)} %convolution_convert_fusion.10), channel_id=1, source_target_pairs={{0,1},{1,0},{2,3},{3,2},{4,5},{5,4},{6,7},{7,6},{8,9},{9,8},{10,11... | collective-permute-start | bytes 2359304 | tf_op jit(solution)/shard_map/ppermute | solution.py:130
  406.8 82.2 %collective-permute-start.12 = (bf16[768,512]{1,0:T(8,128)(2,1)}, bf16[768,512]{1,0:T(8,128)(2,1)}, u32[]{:S(2)}, u32[]{:S(2)}) collective-permute-start(bf16[768,512]{1,0:T(8,128)(2,1)} %convolution_convert_fusion.8), channel_id=1, source_target_pairs={{0,1},{1,0},{2,3},{3,2},{4,5},{5,4},{6,7},{7,6},{8,9},{9,8},{10,11... | collective-permute-start | bytes 2359304 | tf_op jit(solution)/shard_map/ppermute | solution.py:130
  417.5 69.7 %collective-permute-start.11 = (bf16[768,512]{1,0:T(8,128)(2,1)}, bf16[768,512]{1,0:T(8,128)(2,1)}, u32[]{:S(2)}, u32[]{:S(2)}) collective-permute-start(bf16[768,512]{1,0:T(8,128)(2,1)} %add_convert_fusion.6), channel_id=1, source_target_pairs={{0,2},{1,3},{2,0},{3,1},{4,6},{5,7},{6,4},{7,5},{8,10},{9,11},{10,... | collective-permute-start | bytes 2359304 | tf_op jit(solution)/shard_map/ppermute | solution.py:130
  436.9 52.2 %collective-permute-start.14 = (bf16[768,512]{1,0:T(8,128)(2,1)}, bf16[768,512]{1,0:T(8,128)(2,1)}, u32[]{:S(2)}, u32[]{:S(2)}) collective-permute-start(bf16[768,512]{1,0:T(8,128)(2,1)} %add_convert_fusion.5), channel_id=1, source_target_pairs={{0,2},{1,3},{2,0},{3,1},{4,6},{5,7},{6,4},{7,5},{8,10},{9,11},{10,... | collective-permute-start | bytes 2359304 | tf_op jit(solution)/shard_map/ppermute | solution.py:130
  477.9 59.8 %reduce-scatter.8.cloned.1.call-start = ((), (), s32[]{:S(2)}) async-start(), calls=%async_computation.20 | async-start | bytes 1966080 | tf_op jit(solution)/shard_map/reduce_scatter | solution.py:161
  481.7 43.7 %collective-permute-start.15 = (bf16[512,768]{1,0:T(8,128)(2,1)}, bf16[512,768]{1,0:T(8,128)(2,1)}, u32[]{:S(2)}, u32[]{:S(2)}) collective-permute-start(bf16[512,768]{1,0:T(8,128)(2,1)} %convolution_convert_fusion.6), channel_id=1, source_target_pairs={{0,1},{1,0},{2,3},{3,2},{4,5},{5,4},{6,7},{7,6},{8,9},{9,8},{10,11... | collective-permute-start | bytes 2359304 | tf_op jit(solution)/shard_map/ppermute | solution.py:130
  485.6 39.9 %collective-permute-start.17 = (bf16[512,768]{1,0:T(8,128)(2,1)}, bf16[512,768]{1,0:T(8,128)(2,1)}, u32[]{:S(2)}, u32[]{:S(2)}) collective-permute-start(bf16[512,768]{1,0:T(8,128)(2,1)} %add_convert_fusion.4), channel_id=1, source_target_pairs={{0,2},{1,3},{2,0},{3,1},{4,6},{5,7},{6,4},{7,5},{8,10},{9,11},{10,... | collective-permute-start | bytes 2359304 | tf_op jit(solution)/shard_map/ppermute | solution.py:130
  (138 other events, 1284.0 us)
Sparse Core Ops, SparseCore 0:
  9.6 31.5 all-gather.5
  44.7 54.4 all-gather.7
  100.7 23.4 all-gather.13
  126.8 56.3 all-gather.11
  185.2 18.1 all-gather.9
  258.5 29.3 reduce-scatter.5
  314.2 29.3 reduce-scatter.3
  494.9 35.1 reduce-scatter.7

commit v2 on v1

--- a/solution.py
+++ b/solution.py
@@ -1,8 +1,11 @@
+import functools
 import math
 
 import jax
 import jax.numpy as jnp
 from jax import lax
+from jax.experimental import pallas as pl
+from jax.experimental.pallas import tpu as pltpu
 from jax.sharding import PartitionSpec as P
 
 HEAD = 64
@@ -105,16 +108,126 @@
     return grad_query, grad_key, grad_value
 
 
-def branch_forward(rows, w_gate, w_up):
-    gate, up = dot(rows, w_gate), dot(rows, w_up)
-    return gate, up, (jax.nn.silu(gate) * up).astype(LOW)
-
-
-def branch_activation_grads(gate, up, grad_hidden):
-    sigmoid = jax.nn.sigmoid(gate)
-    grad_gate = grad_hidden * up * sigmoid * (1.0 + gate * (1.0 - sigmoid))
-    grad_up = grad_hidden * gate * sigmoid
-    return grad_gate.astype(LOW), grad_up.astype(LOW)
+def branch_rows_kernel(chunks, flipped, x_ref, g_ref, *refs):
+    weights, (hidden_ref, ggate_ref, gup_ref, grad_ref) = refs[: 2 * chunks], refs[2 * chunks :]
+    x, g = x_ref[...], g_ref[...]
+    out_dot = dot if flipped else dot_nt
+    total = None
+    for chunk in range(chunks):
+        w_in, w_out = weights[2 * chunk], weights[2 * chunk + 1]
+        size = w_in.shape[2]
+        at = pl.ds(chunk * size, size)
+        gate, up = dot(x, w_in[0]), dot(x, w_in[1])
+        grad_hidden = out_dot(g, w_out[...])
+        sigmoid = 1.0 / (1.0 + jnp.exp(-gate))
+        active = gate * sigmoid
+        hidden_ref[:, at] = (active * up).astype(LOW)
+        ggate = (grad_hidden * up * sigmoid * (1.0 + gate * (1.0 - sigmoid))).astype(LOW)
+        gup = (grad_hidden * active).astype(LOW)
+        ggate_ref[:, at] = ggate
+        gup_ref[:, at] = gup
+        part = dot_nt(ggate, w_in[0]) + dot_nt(gup, w_in[1])
+        total = part if total is None else total + part
+    grad_ref[...] = total.astype(LOW)
+
+
+def branch_rows(x, g, chunks, flipped):
+    rows, width = x.shape
+    size = chunks[0][0].shape[2]
+    hidden = size * len(chunks)
+    block = math.gcd(rows, 256)
+    row_spec = pl.BlockSpec((block, width), lambda i: (i, 0))
+    hidden_spec = pl.BlockSpec((block, hidden), lambda i: (i, 0))
+    weights = [w for chunk in chunks for w in chunk]
+    whole = [
+        pl.BlockSpec(w.shape, functools.partial(lambda n, i: (0,) * n, w.ndim),
+                     pipeline_mode=pl.Buffered(1))
+        for w in weights
+    ]
+    hidden_type = jax.ShapeDtypeStruct((rows, hidden), LOW)
+    return pl.pallas_call(
+        functools.partial(branch_rows_kernel, len(chunks), flipped),
+        grid=(rows // block,),
+        in_specs=[row_spec, row_spec] + whole,
+        out_specs=[hidden_spec] * 3 + [row_spec],
+        out_shape=[hidden_type] * 3 + [jax.ShapeDtypeStruct((rows, width), LOW)],
+        compiler_params=pltpu.CompilerParams(vmem_limit_bytes=48 * 1024 * 1024),
+        cost_estimate=pl.CostEstimate(
+            flops=10 * rows * width * hidden,
+            bytes_accessed=6 * (width * hidden + rows * hidden + rows * width),
+            transcendentals=rows * hidden,
+        ),
+        name="branch_rows",
+    )(x, g, *weights)
+
+
+def branch_out_kernel(chunks, flipped, hidden_ref, *refs):
+    weights, out_ref = refs[:chunks], refs[chunks]
+    total = None
+    for chunk in range(chunks):
+        w_out = weights[chunk][...]
+        size = w_out.shape[1 if flipped else 0]
+        part = hidden_ref[:, pl.ds(chunk * size, size)]
+        part = dot_nt(part, w_out) if flipped else dot(part, w_out)
+        total = part if total is None else total + part
+    out_ref[...] = total.astype(LOW)
+
+
+def branch_out(hidden, outs, flipped):
+    rows, size = hidden.shape
+    width = outs[0].shape[0 if flipped else 1]
+    block = math.gcd(rows, 256)
+    return pl.pallas_call(
+        functools.partial(branch_out_kernel, len(outs), flipped),
+        grid=(rows // block,),
+        in_specs=[pl.BlockSpec((block, size), lambda i: (i, 0))]
+        + [
+            pl.BlockSpec(w.shape, lambda i: (0, 0), pipeline_mode=pl.Buffered(1)) for w in outs
+        ],
+        out_specs=pl.BlockSpec((block, width), lambda i: (i, 0)),
+        out_shape=jax.ShapeDtypeStruct((rows, width), LOW),
+        compiler_params=pltpu.CompilerParams(vmem_limit_bytes=48 * 1024 * 1024),
+        cost_estimate=pl.CostEstimate(
+            flops=2 * rows * width * size,
+            bytes_accessed=2 * (width * size + rows * size + rows * width),
+            transcendentals=0,
+        ),
+        name="branch_out",
+    )(hidden, *outs)
+
+
+def branch_grads_kernel(x_ref, g_ref, hidden_ref, ggate_ref, gup_ref, in_ref, out_ref):
+    x, g = x_ref[...], g_ref[...]
+    in_ref[0, 0] = dot_tn(x, ggate_ref[...]).astype(LOW)
+    in_ref[0, 1] = dot_tn(x, gup_ref[...]).astype(LOW)
+    out_ref[0] = dot_tn(g, hidden_ref[...]).astype(LOW)
+
+
+def branch_grads(x, g, hidden, ggate, gup, first, chunks, size):
+    rows, width = x.shape
+    block = math.gcd(width, 256)
+    row_spec = pl.BlockSpec((rows, block), lambda j, i: (0, i))
+    hidden_spec = pl.BlockSpec((rows, size), lambda j, i: (0, first + j))
+    return pl.pallas_call(
+        branch_grads_kernel,
+        grid=(chunks, width // block),
+        in_specs=[row_spec, row_spec, hidden_spec, hidden_spec, hidden_spec],
+        out_specs=[
+            pl.BlockSpec((1, 2, block, size), lambda j, i: (j, 0, i, 0)),
+            pl.BlockSpec((1, block, size), lambda j, i: (j, i, 0)),
+        ],
+        out_shape=[
+            jax.ShapeDtypeStruct((chunks, 2, width, size), LOW),
+            jax.ShapeDtypeStruct((chunks, width, size), LOW),
+        ],
+        compiler_params=pltpu.CompilerParams(vmem_limit_bytes=48 * 1024 * 1024),
+        cost_estimate=pl.CostEstimate(
+            flops=6 * rows * width * size * chunks,
+            bytes_accessed=6 * chunks * (width * size + rows * size + rows * width),
+            transcendentals=0,
+        ),
+        name="branch_grads",
+    )(x, g, hidden, ggate, gup)
 
 
 def adam_step(weight, mean_old, square_old, gradient, rate):
@@ -126,41 +239,64 @@
     return (mean_new, square_new, updated)
 
 
-def swap_with(value, mask, count):
-    return lax.ppermute(value, "tensor", [(i, i ^ mask) for i in range(count)])
-
-
-def gather_chunks(parts, count):
+def swap(value, axis, mask, count):
+    return lax.ppermute(value, axis, [(i, i ^ mask) for i in range(count)])
+
+
+def after(value, *earlier):
+    return lax.optimization_barrier((value,) + earlier)[0]
+
+
+def by_rank(parts, rank):
+    count = len(parts)
+    ordered = []
+    for place in range(count):
+        chosen = parts[place]
+        for other in range(1, count):
+            chosen = jnp.where(rank == other, parts[place ^ other], chosen)
+        ordered.append(chosen)
+    return ordered
+
+
+def gather_relative(value, count):
     if count != 4:
-        whole = [lax.all_gather(p, "tensor", axis=0) for p in parts]
-        return [[w[j] for w in whole] for j in range(count)]
-    far = [swap_with(p, 2, count) for p in parts]
-    near = [swap_with(p, 1, count) for p in parts]
-    both = [swap_with(p, 1, count) for p in far]
-    return [parts, near, far, both]
-
-
-def scatter_chunks(chunks, count):
-    parts = range(len(chunks[0]))
-    if count != 4:
-        sums = []
-        for p in parts:
-            stacked = jnp.stack([chunks[j][p].astype(LOW) for j in range(count)])
-            got = lax.all_to_all(stacked, "tensor", split_axis=0, concat_axis=0, tiled=True)
-            sums.append(jnp.sum(got.astype(FULL), axis=0))
-        return sums
-    far = [swap_with(chunks[3][p].astype(LOW), 1, count) for p in parts]
-    near = [swap_with(chunks[1][p].astype(LOW), 1, count) for p in parts]
-    across = [
-        swap_with((chunks[2][p] + far[p].astype(FULL)).astype(LOW), 2, count) for p in parts
-    ]
-    return [chunks[0][p] + near[p].astype(FULL) + across[p].astype(FULL) for p in parts]
-
-
-def sum_rows(terms):
-    return lax.psum_scatter(
-        terms.astype(LOW), "tensor", scatter_dimension=0, tiled=True
-    ).astype(FULL)
+        rank = lax.axis_index("tensor")
+        every = lax.all_gather(value, "tensor", axis=0)
+        return [lax.dynamic_index_in_dim(every, rank ^ m, 0, False) for m in range(count)]
+    far = swap(value, "tensor", 2, count)
+    near = swap(value, "tensor", 1, count)
+    return [value, near, far, swap(far, "tensor", 1, count)]
+
+
+def send_relative(parts):
+    count = len(parts)
+    return [parts[0]] + [swap(parts[m], "tensor", m, count) for m in range(1, count)]
+
+
+def sum_relative(parts):
+    got = send_relative([p.astype(LOW) for p in parts])
+    total = parts[0].astype(FULL)
+    for part in got[1:]:
+        total = total + part.astype(FULL)
+    return total
+
+
+def sum_halving(parts, axis, count):
+    parts = dict(enumerate(parts))
+    mask = 1
+    while mask < count:
+        leaving = [m for m in parts if m & mask]
+        sent = jnp.stack([parts[m].astype(LOW) for m in leaving])
+        got = swap(sent, axis, mask, count).astype(FULL)
+        parts = {
+            m ^ mask: parts[m ^ mask].astype(FULL) + got[at] for at, m in enumerate(leaving)
+        }
+        mask *= 2
+    return parts[0].astype(FULL)
+
+
+def block_of(value, place, size, dim=0):
+    return lax.dynamic_slice_in_dim(value, place * size, size, dim)
 
 
 def exchange(value):
@@ -222,23 +358,23 @@
     w_qkv = got[:, : 3 * head_width]
     gain_pair = got[:, 3 * head_width :].astype(FULL).T
 
-    tokens_all = lax.all_gather(tokens, "tensor", axis=0, tiled=True)
+    tokens_all = jnp.concatenate(by_rank(gather_relative(tokens, count), rank), axis=0)
     w_mix_out = lax.all_gather(
         mixing_out.astype(LOW), ("wide", "tensor"), axis=0, tiled=True
     )
     shared_low = jnp.concatenate(
-        [shared_in.astype(LOW), shared_out.astype(LOW).T[:, None]], axis=1
-    )
-    w_shared = lax.all_gather(shared_low, "wide", axis=0, tiled=True)
-    cotangent_all = lax.all_gather(cotangent, "tensor", axis=0, tiled=True)
-    expert_chunks = gather_chunks(
-        [
-            expert_in[0, :, 0].astype(LOW),
-            expert_in[0, :, 1].astype(LOW),
-            expert_out[0].astype(LOW),
-        ],
-        count,
-    )
+        [shared_in.astype(LOW).transpose(1, 0, 2), shared_out.astype(LOW).T[None]], axis=0
+    )
+    w_shared = lax.all_gather(shared_low, "wide", axis=1, tiled=True)
+    cotangent_rel = jnp.concatenate(gather_relative(cotangent, count), axis=0)
+    expert_chunks = list(
+        zip(
+            gather_relative(expert_in[0].astype(LOW).transpose(1, 0, 2), count),
+            gather_relative(expert_out[0].astype(LOW), count),
+        )
+    )
+    if count == 4:
+        expert_chunks = [expert_chunks[m] for m in (0, 2, 1, 3)]
 
     own_routes = lax.dynamic_slice_in_dim(routes, rank * rows_dev, rows_dev, 0)
     own_logits = lax.dynamic_slice_in_dim(gate_logits, rank * rows_dev, rows_dev, 0)
@@ -255,6 +391,7 @@
     grad_out = cotangent.astype(FULL)
     grad_routes = [(gates[:, k : k + 1] * grad_out).astype(LOW) for k in range(TOP)]
     grad_slots = (dot(picks[0], grad_routes[0]) + dot(picks[1], grad_routes[1])).astype(LOW)
+    grad_slots = after(grad_slots, got)
     expert_grads = exchange(grad_slots.reshape(wide, capacity, width)).reshape(slots, width)
 
     tree_places = jnp.arange(tree_length, dtype=jnp.int32)
@@ -268,76 +405,75 @@
     keys = rotate(projected[:, 1], cosine, sine).astype(LOW)
     values = projected[:, 2].astype(LOW)
     attended, log_totals = attend_forward(queries, keys, values, allowed)
-    attended_low = lax.all_to_all(
-        attended.astype(LOW).reshape(tree_length, head_width),
-        "tensor",
-        split_axis=0,
-        concat_axis=1,
-        tiled=True,
-    )[:, :width]
+    attended = after(attended.astype(LOW).reshape(tree_length, head_width), *expert_chunks[1])
+    attended = send_relative([block_of(attended, rank ^ m, rows_dev) for m in range(count)])
+    attended_low = jnp.concatenate(by_rank(attended, rank), axis=1)[:, :width]
     input_rows = tokens.astype(FULL)
     residual = input_rows + dot(attended_low, w_mix_out)
     factor_two = rms_factor(residual)
     normed_two = (residual * factor_two * gain_pair[1]).astype(LOW)
 
     row_slots = dot(pick_any, normed_two).astype(LOW)
+    row_slots = after(row_slots, expert_grads)
     expert_rows = exchange(row_slots.reshape(wide, capacity, width)).reshape(slots, width)
-    shared_rows = lax.all_gather(normed_two, "tensor", axis=0, tiled=True)
-    sh_gate_w, sh_up_w, sh_out_t = w_shared[:, 0], w_shared[:, 1], w_shared[:, 2]
-    sh_gate, sh_up, sh_hidden = branch_forward(shared_rows, sh_gate_w, sh_up_w)
-    sh_grad_hidden = dot(cotangent_all, sh_out_t)
-    sh_ggate, sh_gup = branch_activation_grads(sh_gate, sh_up, sh_grad_hidden)
-    sh_grad_rows = sum_rows(dot_nt(sh_ggate, sh_gate_w) + dot_nt(sh_gup, sh_up_w))
-    sh_part = sum_rows(dot_nt(sh_hidden, sh_out_t))
-    sh_grads = jnp.stack(
-        [
-            dot_tn(shared_rows, sh_ggate).astype(LOW),
-            dot_tn(shared_rows, sh_gup).astype(LOW),
-            dot_tn(cotangent_all, sh_hidden).astype(LOW),
-        ],
-        axis=1,
-    )
-
-    states = []
-    grad_rows = 0.0
-    for gate_w, up_w, out_w in expert_chunks:
-        gate, up, hidden = branch_forward(expert_rows, gate_w, up_w)
-        ggate, gup = branch_activation_grads(gate, up, dot_nt(expert_grads, out_w))
-        grad_rows = grad_rows + dot_nt(ggate, gate_w) + dot_nt(gup, up_w)
-        states.append((hidden, ggate, gup))
-    back_rows = exchange(grad_rows.astype(LOW).reshape(wide, capacity, width))
-    back_rows = back_rows.reshape(slots, width)
-    out_rows = 0.0
-    for (hidden, _, _), (_, _, out_w) in zip(states, expert_chunks):
-        out_rows = out_rows + dot(hidden, out_w)
-    returned = exchange(out_rows.astype(LOW).reshape(wide, capacity, width))
-    returned = returned.reshape(slots, width)
-    weight_grads = [
-        [dot_tn(expert_rows, ggate), dot_tn(expert_rows, gup), dot_tn(hidden, expert_grads)]
-        for hidden, ggate, gup in states
-    ]
-    grad_ex_gate, grad_ex_up, grad_ex_out = scatter_chunks(weight_grads, count)
-    grad_ex_in = jnp.stack([grad_ex_gate, grad_ex_up], axis=1)
+    shared_rows = jnp.concatenate(gather_relative(normed_two, count), axis=0)
+    shared_chunk = (w_shared[:2], w_shared[2])
+    sh_hidden, sh_ggate, sh_gup, sh_grad_rows = branch_rows(
+        shared_rows, cotangent_rel, [shared_chunk], True
+    )
+    sh_grad_rows = sum_relative(jnp.split(sh_grad_rows, count))
+    sh_part = branch_out(sh_hidden, [shared_chunk[1]], True)
+    sh_size = sh_hidden.shape[1]
+    sh_grad_in, sh_grad_out = branch_grads(
+        shared_rows, cotangent_rel, sh_hidden, sh_ggate, sh_gup, 0, 1, sh_size
+    )
+
+    ex_hidden, ex_ggate, ex_gup, ex_grad_rows = branch_rows(
+        expert_rows, expert_grads, expert_chunks, False
+    )
+    back_rows = exchange(ex_grad_rows.reshape(wide, capacity, width)).reshape(slots, width)
+    out_rows = branch_out(ex_hidden, [chunk[1] for chunk in expert_chunks], False)
+    out_rows = after(out_rows, back_rows)
+    returned = exchange(out_rows.reshape(wide, capacity, width)).reshape(slots, width)
+    ex_size = ex_hidden.shape[1] // count
+    ex_grads = functools.partial(
+        branch_grads, expert_rows, expert_grads, ex_hidden, ex_ggate, ex_gup
+    )
+    if count == 4:
+        sent = [swap(part, "tensor", 1, count).astype(FULL) for part in ex_grads(2, 2, ex_size)]
+        kept = ex_grads(0, 2, ex_size)
+        across = [
+            swap((part[1] + got[1]).astype(LOW), "tensor", 2, count)
+            for part, got in zip(kept, sent)
+        ]
+        grad_ex_in, grad_ex_out = [
+            part[0] + got[0] + far.astype(FULL) for part, got, far in zip(kept, sent, across)
+        ]
+    else:
+        grad_ex_in, grad_ex_out = [sum_relative(list(part)) for part in ex_grads(0, count, ex_size)]
+    grad_ex_in = grad_ex_in.transpose(1, 0, 2)
+    grad_ex_out = grad_ex_out.T
 
     grad_normed_two = dot_tn(pick_any, back_rows) + sh_grad_rows
     grad_part, hat_two = rms_back(residual, factor_two, gain_pair[1], grad_normed_two)
     gain_two_part = jnp.sum(grad_normed_two * hat_two, axis=0)
     grad_residual = grad_out + grad_part
     grad_res_low = grad_residual.astype(LOW)
-    grad_attended = dot_nt(grad_res_low, w_mix_out).astype(LOW)
-    grad_attended = jnp.pad(grad_attended, ((0, 0), (0, head_pad * HEAD)))
-    grad_attended = lax.all_to_all(
-        grad_attended, "tensor", split_axis=1, concat_axis=0, tiled=True
-    ).reshape(tree_length, heads_dev, HEAD)
-    grad_mix_out = dot_tn(attended_low, grad_res_low).astype(LOW)
-    grad_mix_out = lax.all_to_all(
-        grad_mix_out.reshape(wide * count, rows_weight, width),
-        ("wide", "tensor"),
-        split_axis=0,
-        concat_axis=0,
-        tiled=True,
-    )
-    grad_mix_out = jnp.sum(grad_mix_out.astype(FULL), axis=0)
+    w_mix_pad = jnp.pad(w_mix_out, ((0, head_pad * HEAD), (0, 0)))
+    grad_attended = send_relative(
+        [
+            dot_nt(grad_res_low, block_of(w_mix_pad, rank ^ m, head_width)).astype(LOW)
+            for m in range(count)
+        ]
+    )
+    grad_attended = jnp.concatenate(by_rank(grad_attended, rank), axis=0)
+    grad_attended = grad_attended.reshape(tree_length, heads_dev, HEAD)
+    grad_mix_out = dot_tn(attended_low, grad_res_low).reshape(wide, count, rows_weight, width)
+    grad_mix_out = sum_relative(
+        [lax.dynamic_index_in_dim(grad_mix_out, rank ^ m, 1, False) for m in range(count)]
+    )
+    grad_mix_out = after(grad_mix_out.astype(LOW), returned)
+    grad_mix_out = jnp.sum(exchange(grad_mix_out).astype(FULL), axis=0)
 
     grad_query, grad_key, grad_value = attend_backward(
         queries, keys, values, allowed, grad_attended, log_totals
@@ -346,7 +482,10 @@
         [rotate(grad_query, cosine, -sine), rotate(grad_key, cosine, -sine), grad_value], axis=1
     )
     grad_projected = grad_projected.astype(LOW).reshape(tree_length, 3 * head_width)
-    grad_normed_one = sum_rows(dot_nt(grad_projected, w_qkv))
+    grad_normed_one = dot_nt(grad_projected, w_qkv).astype(LOW)
+    grad_normed_one = sum_relative(
+        [block_of(grad_normed_one, rank ^ m, rows_dev) for m in range(count)]
+    )
     grad_mix_in = dot_tn(normed_one, grad_projected).astype(LOW)
     sent = jnp.concatenate([grad_mix_in, gain_two_part.astype(LOW)[:, None]], axis=1)
     got = lax.all_to_all(
@@ -368,14 +507,17 @@
     input_grad = grad_residual + grad_part
 
     per_route = [dot_tn(picks[k], returned) for k in range(TOP)]
-    mixed = (
-        residual + gates[:, :1] * per_route[0] + gates[:, 1:] * per_route[1] + sh_part
-    )
+    sh_part = sum_relative(jnp.split(sh_part, count))
+    mixed = residual + gates[:, :1] * per_route[0] + gates[:, 1:] * per_route[1] + sh_part
     gate_grad = jnp.stack([jnp.sum(grad_out * rows, axis=-1) for rows in per_route], axis=1)
     logit_grad = gates * (gate_grad - jnp.sum(gates * gate_grad, axis=-1, keepdims=True))
 
-    sh_grads = exchange(sh_grads.reshape(wide, width // wide, 3, -1))
-    sh_grads = jnp.sum(sh_grads.astype(FULL), axis=0)
+    tree = lax.axis_index("wide")
+    rows_shared = width // wide
+    sh_grads = jnp.concatenate([sh_grad_in[0], sh_grad_out], axis=0)
+    sh_grads = sum_halving(
+        [block_of(sh_grads, tree ^ m, rows_shared, 1) for m in range(wide)], "wide", wide
+    )
 
     weights = (mixing_in, mixing_out, norm_gains, shared_in, shared_out, expert_in, expert_out)
     means = (
@@ -400,8 +542,8 @@
         grad_mix_in,
         grad_mix_out,
         jnp.stack([grad_gain_one, grad_gain_two]),
-        sh_grads[:, :2],
-        sh_grads[:, 2].T,
+        sh_grads[:2].transpose(1, 0, 2),
+        sh_grads[2].T,
         grad_ex_in[None],
         grad_ex_out[None],
     )

time: 559 us -> 494 us (0.88)
  the two profiles are of different devices: /device:TPU:0 before, /device:TPU:3 now
where the time goes in v2:
time: 494 us; the launch traced here: 485 us
  waiting for transfers between devices  151 us (31%)
  local copies, waits for them, and re-layouts  72.3 us (15%)
  starting transfers between devices  67.2 us (14%)
  Pallas kernels  66.9 us (14%)
  other arithmetic  64.9 us (13%)
  matrix products  47.2 us (10%)
  between operations  16.1 us (3%)
    ppermute x40, waiting for transfers between devices, swap(): return lax.ppermute(value, axis, [(i, i ^ mask) for i in range(count)])  118 us
    unnamed x242, local copies, waits for them, and re-layouts  54.9 us
    ppermute x40, starting transfers between devices, swap(): return lax.ppermute(value, axis, [(i, i ^ mask) for i in range(count)])  32.9 us
    pallas_call x2, Pallas kernels, branch_rows(): pl.pallas_call(functools.partial(branch_rows_kernel, len(chunks), flipped...  32.1 us
    all_gather x1, waiting for transfers between devices, body(): w_shared = lax.all_gather(shared_low, 'wide', axis=1, tiled=True)  28.3 us
    pallas_call x3, Pallas kernels, branch_grads(): pl.pallas_call(branch_grads_kernel, grid=(chunks, width // block), in_spe...  26.7 us
    all_to_all x5, starting transfers between devices, exchange(): lax.all_to_all(value, 'wide', split_axis=0, concat_axis=0, tiled=True)  22.9 us
    sub x7, other arithmetic, adam_step(): weight - rate * (mean_hat / (jnp.sqrt(square_hat) + ADAM_EPS) + DECAY * w...  12.5 us
  transfers between devices with their start and end apart: 49, of which 13 were waited for; matrix products, arithmetic and copies ran while one was open for 33% of the time, Pallas kernels for 14%

profile of v2, /device:TPU:3, one launch (start us, length us, event | category | flops | bytes accessed | tf_op | source)
XLA Modules:
  0.0 485.4 jit_solution(7285287601511474182)
XLA Ops:
  12.9 6.4 %all-to-all-start = ((bf16[32,24,578]{2,1,0:T(8,128)(2,1)}), bf16[32,24,578]{2,1,0:T(8,128)(2,1)}, u32[]{:S(2)}, u32[]{:S(2)}) async-start(bf16[32,24,578]{2,1,0:T(8,128)(2,1)} %bitcast.273), calls=%async_computation | async-start | bytes 1966080 | tf_op jit(solution)/shard_map/all_to_all | solution.py:356
  66.7 18.7 %collective-permute-done.3.refs_2_ = bf16[2,768,512]{2,1,0:T(8,128)(2,1)} collective-permute-done((bf16[2,768,512]{2,1,0:T(8,128)(2,1)}, bf16[2,768,512]{2,1,0:T(8,128)(2,1)}, u32[]{:S(2)}, u32[]{:S(2)}) %collective-permute-start.3) | collective-permute-done | bytes 1572896 | tf_op jit(solution)/shard_map/ppermute | solution.py:243
  97.5 5.7 %all-to-all-start.2 = ((bf16[8,128,768]{2,1,0:T(8,128)(2,1)}), bf16[8,128,768]{2,1,0:T(8,128)(2,1)}, u32[]{:S(2)}, u32[]{:S(2)}) async-start(bf16[8,128,768]{2,1,0:T(8,128)(2,1)} %bitcast.277), calls=%async_computation.2 | async-start | bytes 3145728 | tf_op jit(solution)/shard_map/all_to_all | solution.py:303
  106.1 7.2 %collective-permute-done.16 = bf16[256,768]{1,0:T(8,128)(2,1)} collective-permute-done((bf16[256,768]{1,0:T(8,128)(2,1)S(1)}, bf16[256,768]{1,0:T(8,128)(2,1)}, u32[]{:S(2)}, u32[]{:S(2)}) %collective-permute-start.16) | collective-permute-done | bytes 393248 | tf_op jit(solution)/shard_map/ppermute | solution.py:243
  116.7 5.0 %collective-permute-done.13 = bf16[256,768]{1,0:T(8,128)(2,1)S(1)} collective-permute-done((bf16[256,768]{1,0:T(8,128)(2,1)S(1)}, bf16[256,768]{1,0:T(8,128)(2,1)S(1)}, u32[]{:S(2)}, u32[]{:S(2)}) %collective-permute-start.13) | collective-permute-done | bytes 393248 | tf_op jit(solution)/shard_map/ppermute | solution.py:243
  131.1 28.3 %all-gather.5.cloned.1.call-done = bf16[3,768,512]{2,1,0:T(8,128)(2,1)} async-done(((bf16[3,96,512]{2,1,0:T(8,128)(2,1)}), bf16[3,768,512]{2,1,0:T(8,128)(2,1)}) %all-gather.5.cloned.1.call-update) | async-done | bytes 2359312 | tf_op jit(solution)/shard_map/all_gather | solution.py:368
  163.3 7.6 %branch_rows.3 = (bf16[1024,512]{1,0:T(8,128)(2,1)S(1)}, bf16[1024,512]{1,0:T(8,128)(2,1)S(1)}, bf16[1024,512]{1,0:T(8,128)(2,1)S(1)}, bf16[1024,768]{1,0:T(8,128)(2,1)S(1)}) custom-call(bf16[1024,768]{1,0:T(8,128)(2,1)} %pad_maximum_fusion.1.x_ref, bf16[1024,768]{1,0:T(8,128)(2,1)} %constant_dynamic-update-slice_fusion.g_ref, ...), custom_call_target="tpu_custom_call" | custom-call | flops 4026531840 | bytes 10223616 | tf_op jit(solution)/shard_map/branch_rows/pallas_call | solution.py:148
  172.1 4.9 %branch_grads.3 = (bf16[1,2,768,512]{3,2,1,0:T(8,128)(2,1)S(1)}, bf16[1,768,512]{2,1,0:T(8,128)(2,1)S(1)}) custom-call(bf16[1024,768]{1,0:T(8,128)(2,1)} %pad_maximum_fusion.1.x_ref, bf16[1024,768]{1,0:T(8,128)(2,1)} %constant_dynamic-update-slice_fusion.g_ref, bf16[1024,512]{1,0:T(8,128)(2,1)S(1)} %get-tuple-element.49.hidden_ref, ...), custom_call_target="tpu_custom_call" | custom-call | flops 2415919104 | bytes 10223616 | tf_op jit(solution)/shard_map/branch_grads/pallas_call | solution.py:211
  178.3 24.5 %branch_rows.2 = (bf16[1024,2048]{1,0:T(8,128)(2,1)}, bf16[1024,2048]{1,0:T(8,128)(2,1)}, bf16[1024,2048]{1,0:T(8,128)(2,1)}, bf16[1024,768]{1,0:T(8,128)(2,1)S(1)}) custom-call(bf16[1024,768]{1,0:T(8,128)(2,1)} %bitcast.20.x_ref, bf16[1024,768]{1,0:T(8,128)(2,1)} %bitcast.261, bf16[2,768,512]{2,1,0:T(8,128)(2,1)} %bitcast.253.refs_0_, ...), custom_call_target="tpu_custom_call" | custom-call | flops 16106127360 | bytes 26738688 | tf_op jit(solution)/shard_map/branch_rows/pallas_call | solution.py:148
  203.9 4.3 all-to-all-start.3
  224.4 11.2 %branch_grads.5 = (bf16[2,2,768,512]{3,2,1,0:T(8,128)(2,1)}, bf16[2,768,512]{2,1,0:T(8,128)(2,1)}) custom-call(bf16[1024,768]{1,0:T(8,128)(2,1)} %bitcast.20.x_ref, bf16[1024,768]{1,0:T(8,128)(2,1)S(1)} %bitcast.262, bf16[1024,2048]{1,0:T(8,128)(2,1)} %get-tuple-element.46.hidden_ref, bf16[1024,2048]{1,0:T(8,128)(2,1)} %get-tuple-element.56.ggate_ref, ...), custom_call_target="tpu_custom_call" | custom-call | flops 4831838208 | bytes 20447232 | tf_op jit(solution)/shard_map/branch_grads/pallas_call | solution.py:211
  243.2 6.2 %collective-permute-done.34 = bf16[2,3,96,512]{3,2,1,0:T(8,128)(2,1)S(1)} collective-permute-done((bf16[2,3,96,512]{3,2,1,0:T(8,128)(2,1)S(1)}, bf16[2,3,96,512]{3,2,1,0:T(8,128)(2,1)S(1)}, u32[]{:S(2)}, u32[]{:S(2)}) %collective-permute-start.34) | collective-permute-done | bytes 589856 | tf_op jit(solution)/shard_map/ppermute | solution.py:243
  250.6 6.4 %branch_out.2 = bf16[1024,768]{1,0:T(8,128)(2,1)S(1)} custom-call(bf16[1024,2048]{1,0:T(8,128)(2,1)} %get-tuple-element.46.hidden_ref, bf16[512,768]{1,0:T(8,128)(2,1)} %convert_bitcast_fusion.refs_1_.refs_0_, bf16[512,768]{1,0:T(8,128)(2,1)} %collective-permute-done.4.refs_3_.refs_1_, bf16[512,768]{1,0:T(8,128)(2,1)} %collective-permute-done.9.refs_5_.refs_2_, ...), custom_call_target="tpu_custom_call" | custom-call | flops 3221225472 | bytes 8912896 | tf_op jit(solution)/shard_map/branch_out/pallas_call | solution.py:180
  258.2 4.5 all-to-all-start.4
  264.1 10.7 %branch_grads.4 = (bf16[2,2,768,512]{3,2,1,0:T(8,128)(2,1)}, bf16[2,768,512]{2,1,0:T(8,128)(2,1)S(1)}) custom-call(bf16[1024,768]{1,0:T(8,128)(2,1)} %bitcast.20.x_ref, bf16[1024,768]{1,0:T(8,128)(2,1)S(1)} %bitcast.263, bf16[1024,2048]{1,0:T(8,128)(2,1)} %get-tuple-element.46.hidden_ref, bf16[1024,2048]{1,0:T(8,128)(2,1)} %get-tuple-element.56.ggate_ref, ...), custom_call_target="tpu_custom_call" | custom-call | flops 4831838208 | bytes 20447232 | tf_op jit(solution)/shard_map/branch_grads/pallas_call | solution.py:211
  279.2 32.6 %collective-permute-done.35 = bf16[1,3,96,512]{3,2,1,0:T(8,128)(2,1)S(1)} collective-permute-done((bf16[1,3,96,512]{3,2,1,0:T(8,128)(2,1)S(1)}, bf16[1,3,96,512]{3,2,1,0:T(8,128)(2,1)S(1)}, u32[]{:S(2)}, u32[]{:S(2)}) %collective-permute-start.35) | collective-permute-done | bytes 294944 | tf_op jit(solution)/shard_map/ppermute | solution.py:243
  318.0 11.4 %collective-permute-done.39 = bf16[768,512]{1,0:T(8,128)(2,1)S(1)} collective-permute-done((bf16[768,512]{1,0:T(8,128)(2,1)S(1)}, bf16[768,512]{1,0:T(8,128)(2,1)S(1)}, u32[]{:S(2)}, u32[]{:S(2)}) %collective-permute-start.39) | collective-permute-done | bytes 786464 | tf_op jit(solution)/shard_map/ppermute | solution.py:243
  354.5 5.8 %collective-permute-done.20 = bf16[256,768]{1,0:T(8,128)(2,1)S(1)} collective-permute-done((bf16[256,768]{1,0:T(8,128)(2,1)}, bf16[256,768]{1,0:T(8,128)(2,1)S(1)}, u32[]{:S(2)}, u32[]{:S(2)}) %collective-permute-start.20) | collective-permute-done | bytes 393248 | tf_op jit(solution)/shard_map/ppermute | solution.py:243
  369.9 25.8 %collective-permute-done.25 = bf16[256,192]{0,1:T(8,128)(2,1)S(1)} collective-permute-done((bf16[256,192]{0,1:T(8,128)(2,1)S(1)}, bf16[256,192]{0,1:T(8,128)(2,1)S(1)}, u32[]{:S(2)}, u32[]{:S(2)}) %collective-permute-start.25) | collective-permute-done | bytes 98336 | tf_op jit(solution)/shard_map/ppermute | solution.py:243
  398.9 6.5 %multiply_reduce_fusion = (f32[3,1024]{1,0:T(4,128)S(1)}, f32[3,1024,1024]{1,2,0:T(8,128)S(1)}) fusion(f32[3,1024,1024]{1,2,0:T(8,128)} %copy-done.12, f32[3,1024]{1,0:T(4,128)S(1)} %copy-done.49, bf16[1024,3,64]{0,2,1:T(8,128)(2,1)S(1)} %bitcast.270, f32[1024,3,3,64]{0,3,2,1:T(8,128)} %bitcast.276), kind=kOutput, calls=%fused_computation.1 | convolution fusion | flops 412087296 | bytes 25976832 | tf_op jit(solution)/shard_map/qhd,khd->hqk/dot_general | solution.py:100
  407.3 5.3 %multiply_convert_fusion = bf16[3,1024,1024]{1,2,0:T(8,128)(2,1)} fusion(f32[3,1024,1024]{1,2,0:T(8,128)S(1)} %get-tuple-element.248, f32[3,1024,1024]{1,2,0:T(8,128)S(1)} %bitcast.267, f32[3,1024]{1,0:T(4,128)S(1)} %get-tuple-element.247, f32[3,1024]{1,0:T(4,128)S(1)} %copy-done.49), kind=kLoop, calls=%fused_computation | loop fusion | flops 12582912 | bytes 31481856 | tf_op jit(solution)/shard_map/convert_element_type | solution.py:102
  412.6 5.1 %fusion.27 = f32[1024,3,64]{0,2,1:T(8,128)S(1)} fusion(bf16[3,1024,1024]{1,2,0:T(8,128)(2,1)} %multiply_convert_fusion, bf16[1024,3,32]{0,2,1:T(8,128)(2,1)} %copy-done.61, bf16[1024,3,32]{0,2,1:T(8,128)(2,1)S(1)} %copy-done.60), kind=kOutput, calls=%fused_computation.77 | convolution fusion | flops 403636224 | bytes 7471104 | tf_op jit(solution)/shard_map/hqk,qhd->khd/dot_general | solution.py:104
  443.5 4.9 %all-to-all-start.5 = ((bf16[32,24,577]{2,1,0:T(8,128)(2,1)}), bf16[32,24,577]{2,1,0:T(8,128)(2,1)}, u32[]{:S(2)}, u32[]{:S(2)}) async-start(bf16[32,24,577]{2,1,0:T(8,128)(2,1)} %pad_maximum_fusion.4), calls=%async_computation.5 | async-start | bytes 1966080 | tf_op jit(solution)/shard_map/all_to_all | solution.py:491
  448.5 6.4 %multiply_subtract_fusion = (f32[1,768,2,512]{3,1,2,0:T(8,128)S(1)}, f32[1,768,2,512]{3,1,2,0:T(8,128)S(1)}, f32[1,768,2,512]{3,1,2,0:T(8,128)S(1)}) fusion(f32[1,768,2,512]{3,2,1,0:T(2,128)S(1)} %copy-done.16, bf16[2,768,512]{2,1,0:T(8,128)(2,1)} %collective-permute-done.37, f32[2,2,768,512]{3,2,1,0:T(8,128)} %copy-done.14, ...), kind=kLoop, calls=%fused_computation.48 | loop fusion | flops 14155776 | bytes 25165824 | tf_op jit(solution)/shard_map/sub | solution.py:238
  (444 shorter events, 214.1 us)
Async XLA Ops:
  7.2 85.6 %all-gather.3.cloned.1.call-start = ((), (), s32[]{:S(2)}) async-start(), calls=%async_computation.7 | async-start | bytes 1216512 | tf_op jit(solution)/shard_map/all_gather | solution.py:362
  12.9 31.6 %all-to-all-start = ((bf16[32,24,578]{2,1,0:T(8,128)(2,1)}), bf16[32,24,578]{2,1,0:T(8,128)(2,1)}, u32[]{:S(2)}, u32[]{:S(2)}) async-start(bf16[32,24,578]{2,1,0:T(8,128)(2,1)} %bitcast.273), calls=%async_computation | async-start | bytes 1966080 | tf_op jit(solution)/shard_map/all_to_all | solution.py:356
  19.3 140.1 %all-gather.5.cloned.1.call-start = ((), (), s32[]{:S(2)}) async-start(), calls=%async_computation.8 | async-start | bytes 2654208 | tf_op jit(solution)/shard_map/all_gather | solution.py:368
  21.7 44.9 %collective-permute-start.4 = (bf16[512,768]{1,0:T(8,128)(2,1)}, bf16[512,768]{1,0:T(8,128)(2,1)}, u32[]{:S(2)}, u32[]{:S(2)}) collective-permute-start(bf16[512,768]{1,0:T(8,128)(2,1)} %convert_bitcast_fusion.refs_1_.refs_0_), channel_id=1, source_target_pairs={{0,2},{1,3},{2,0},{3,1},{4,6},{5,7},{6,4},{7,5},{8,10},{9,11},{10,... | collective-permute-start | bytes 2359304 | tf_op jit(solution)/shard_map/ppermute | solution.py:243
  23.4 61.9 %collective-permute-start.3 = (bf16[2,768,512]{2,1,0:T(8,128)(2,1)}, bf16[2,768,512]{2,1,0:T(8,128)(2,1)}, u32[]{:S(2)}, u32[]{:S(2)}) collective-permute-start(bf16[2,768,512]{2,1,0:T(8,128)(2,1)} %bitcast.253.refs_0_), channel_id=1, source_target_pairs={{0,2},{1,3},{2,0},{3,1},{4,6},{5,7},{6,4},{7,5},{8,10},{9,11},{10,... | collective-permute-start | bytes 4718600 | tf_op jit(solution)/shard_map/ppermute | solution.py:243
  50.1 47.4 %all-to-all-start.1 = ((bf16[8,128,768]{2,1,0:T(8,128)(2,1)}), bf16[8,128,768]{2,1,0:T(8,128)(2,1)S(1)}, u32[]{:S(2)}, u32[]{:S(2)}) async-start(bf16[8,128,768]{2,1,0:T(8,128)(2,1)} %bitcast.17), calls=%async_computation.1 | async-start | bytes 3145728 | tf_op jit(solution)/shard_map/all_to_all | solution.py:303
  97.5 80.8 %all-to-all-start.2 = ((bf16[8,128,768]{2,1,0:T(8,128)(2,1)}), bf16[8,128,768]{2,1,0:T(8,128)(2,1)}, u32[]{:S(2)}, u32[]{:S(2)}) async-start(bf16[8,128,768]{2,1,0:T(8,128)(2,1)} %bitcast.277), calls=%async_computation.2 | async-start | bytes 3145728 | tf_op jit(solution)/shard_map/all_to_all | solution.py:303
  116.2 62.1 %collective-permute-start.8 = (bf16[2,768,512]{2,1,0:T(8,128)(2,1)}, bf16[2,768,512]{2,1,0:T(8,128)(2,1)}, u32[]{:S(2)}, u32[]{:S(2)}) collective-permute-start(bf16[2,768,512]{2,1,0:T(8,128)(2,1)} %bitcast.253.refs_0_), channel_id=1, source_target_pairs={{0,1},{1,0},{2,3},{3,2},{4,5},{5,4},{6,7},{7,6},{8,9},{9,8},{10,11... | collective-permute-start | bytes 4718600 | tf_op jit(solution)/shard_map/ppermute | solution.py:243
  124.1 54.2 %collective-permute-start.10 = (bf16[2,768,512]{2,1,0:T(8,128)(2,1)}, bf16[2,768,512]{2,1,0:T(8,128)(2,1)}, u32[]{:S(2)}, u32[]{:S(2)}) collective-permute-start(bf16[2,768,512]{2,1,0:T(8,128)(2,1)} %collective-permute-done.3.refs_2_), channel_id=1, source_target_pairs={{0,1},{1,0},{2,3},{3,2},{4,5},{5,4},{6,7},{7,6},{8,9},{9,8},{10,11... | collective-permute-start | bytes 4718600 | tf_op jit(solution)/shard_map/ppermute | solution.py:243
  127.6 50.7 %collective-permute-start.9 = (bf16[512,768]{1,0:T(8,128)(2,1)}, bf16[512,768]{1,0:T(8,128)(2,1)}, u32[]{:S(2)}, u32[]{:S(2)}) collective-permute-start(bf16[512,768]{1,0:T(8,128)(2,1)} %convert_bitcast_fusion.refs_1_.refs_0_), channel_id=1, source_target_pairs={{0,1},{1,0},{2,3},{3,2},{4,5},{5,4},{6,7},{7,6},{8,9},{9,8},{10,11... | collective-permute-start | bytes 2359304 | tf_op jit(solution)/shard_map/ppermute | solution.py:243
  129.9 48.4 %collective-permute-start.11 = (bf16[512,768]{1,0:T(8,128)(2,1)}, bf16[512,768]{1,0:T(8,128)(2,1)}, u32[]{:S(2)}, u32[]{:S(2)}) collective-permute-start(bf16[512,768]{1,0:T(8,128)(2,1)} %collective-permute-done.4.refs_3_.refs_1_), channel_id=1, source_target_pairs={{0,1},{1,0},{2,3},{3,2},{4,5},{5,4},{6,7},{7,6},{8,9},{9,8},{10,11... | collective-permute-start | bytes 2359304 | tf_op jit(solution)/shard_map/ppermute | solution.py:243
  178.3 42.2 %collective-permute-start.33 = (bf16[4,3,96,512]{3,2,1,0:T(8,128)(2,1)}, bf16[4,3,96,512]{3,2,1,0:T(8,128)(2,1)}, u32[]{:S(2)}, u32[]{:S(2)}) collective-permute-start(bf16[4,3,96,512]{3,2,1,0:T(8,128)(2,1)} %pad_maximum_fusion.3), channel_id=1, source_target_pairs={{0,4},{4,0},{8,12},{12,8},{16,20},{20,16},{24,28},{28,24},{1,5},{5... | collective-permute-start | bytes 3538952 | tf_op jit(solution)/shard_map/ppermute | solution.py:243
  203.9 54.3 %all-to-all-start.3 = ((bf16[8,128,768]{2,1,0:T(8,128)(2,1)}), bf16[8,128,768]{2,1,0:T(8,128)(2,1)}, u32[]{:S(2)}, u32[]{:S(2)}) async-start(bf16[8,128,768]{2,1,0:T(8,128)(2,1)} %bitcast.264), calls=%async_computation.3 | async-start | bytes 3145728 | tf_op jit(solution)/shard_map/all_to_all | solution.py:303
  235.5 39.2 %collective-permute-start.38 = (bf16[2,768,512]{2,1,0:T(8,128)(2,1)}, bf16[2,768,512]{2,1,0:T(8,128)(2,1)}, u32[]{:S(2)}, u32[]{:S(2)}) collective-permute-start(bf16[2,768,512]{2,1,0:T(8,128)(2,1)} %get-tuple-element.61), channel_id=1, source_target_pairs={{0,1},{1,0},{2,3},{3,2},{4,5},{5,4},{6,7},{7,6},{8,9},{9,8},{10,11... | collective-permute-start | bytes 4718600 | tf_op jit(solution)/shard_map/ppermute | solution.py:243
  237.2 103.3 %collective-permute-start.21 = (bf16[256,768]{1,0:T(8,128)(2,1)}, bf16[256,768]{1,0:T(8,128)(2,1)}, u32[]{:S(2)}, u32[]{:S(2)}) collective-permute-start(bf16[256,768]{1,0:T(8,128)(2,1)} %get-tuple-element.203), channel_id=1, source_target_pairs={{0,1},{1,0},{2,3},{3,2},{4,5},{5,4},{6,7},{7,6},{8,9},{9,8},{10,11... | collective-permute-start | bytes 1179656 | tf_op jit(solution)/shard_map/ppermute | solution.py:243
  237.2 103.7 %collective-permute-start.22 = (bf16[256,768]{1,0:T(8,128)(2,1)}, bf16[256,768]{1,0:T(8,128)(2,1)}, u32[]{:S(2)}, u32[]{:S(2)}) collective-permute-start(bf16[256,768]{1,0:T(8,128)(2,1)} %get-tuple-element.205), channel_id=1, source_target_pairs={{0,2},{1,3},{2,0},{3,1},{4,6},{5,7},{6,4},{7,5},{8,10},{9,11},{10,... | collective-permute-start | bytes 1179656 | tf_op jit(solution)/shard_map/ppermute | solution.py:243
  238.2 103.9 %collective-permute-start.23 = (bf16[256,768]{1,0:T(8,128)(2,1)}, bf16[256,768]{1,0:T(8,128)(2,1)}, u32[]{:S(2)}, u32[]{:S(2)}) collective-permute-start(bf16[256,768]{1,0:T(8,128)(2,1)} %get-tuple-element.204), channel_id=1, source_target_pairs={{0,3},{1,2},{2,1},{3,0},{4,7},{5,6},{6,5},{7,4},{8,11},{9,10},{10,... | collective-permute-start | bytes 1179656 | tf_op jit(solution)/shard_map/ppermute | solution.py:243
  249.5 96.5 %collective-permute-start.36 = (bf16[2,2,768,512]{3,2,1,0:T(8,128)(2,1)}, bf16[2,2,768,512]{3,2,1,0:T(8,128)(2,1)}, u32[]{:S(2)}, u32[]{:S(2)}) collective-permute-start(bf16[2,2,768,512]{3,2,1,0:T(8,128)(2,1)} %get-tuple-element.59), channel_id=1, source_target_pairs={{0,1},{1,0},{2,3},{3,2},{4,5},{5,4},{6,7},{7,6},{8,9},{9,8},{10,11... | collective-permute-start | bytes 9437192 | tf_op jit(solution)/shard_map/ppermute | solution.py:243
  258.2 94.2 %all-to-all-start.4 = ((bf16[8,128,768]{2,1,0:T(8,128)(2,1)}), bf16[8,128,768]{2,1,0:T(8,128)(2,1)}, u32[]{:S(2)}, u32[]{:S(2)}) async-start(bf16[8,128,768]{2,1,0:T(8,128)(2,1)} %bitcast.265), calls=%async_computation.4 | async-start | bytes 3145728 | tf_op jit(solution)/shard_map/all_to_all | solution.py:303
  274.7 37.0 %collective-permute-start.35 = (bf16[1,3,96,512]{3,2,1,0:T(8,128)(2,1)S(1)}, bf16[1,3,96,512]{3,2,1,0:T(8,128)(2,1)S(1)}, u32[]{:S(2)}, u32[]{:S(2)}) collective-permute-start(bf16[1,3,96,512]{3,2,1,0:T(8,128)(2,1)S(1)} %fusion.111), channel_id=1, source_target_pairs={{0,16},{4,20},{8,24},{12,28},{16,0},{20,4},{24,8},{28,12},{1,17},{... | collective-permute-start | bytes 884744 | tf_op jit(solution)/shard_map/ppermute | solution.py:243
  352.0 96.5 %collective-permute-start.37 = (bf16[2,768,512]{2,1,0:T(8,128)(2,1)}, bf16[2,768,512]{2,1,0:T(8,128)(2,1)}, u32[]{:S(2)}, u32[]{:S(2)}) collective-permute-start(bf16[2,768,512]{2,1,0:T(8,128)(2,1)} %fusion.22), channel_id=1, source_target_pairs={{0,2},{1,3},{2,0},{3,1},{4,6},{5,7},{6,4},{7,5},{8,10},{9,11},{10,... | collective-permute-start | bytes 4718600 | tf_op jit(solution)/shard_map/ppermute | solution.py:243
  369.7 57.7 %collective-permute-start.30 = (bf16[8,24,768]{2,1,0:T(8,128)(2,1)}, bf16[8,24,768]{2,1,0:T(8,128)(2,1)}, u32[]{:S(2)}, u32[]{:S(2)}) collective-permute-start(bf16[8,24,768]{2,1,0:T(8,128)(2,1)} %get-tuple-element.194), channel_id=1, source_target_pairs={{0,1},{1,0},{2,3},{3,2},{4,5},{5,4},{6,7},{7,6},{8,9},{9,8},{10,11... | collective-permute-start | bytes 884744 | tf_op jit(solution)/shard_map/ppermute | solution.py:243
  395.6 31.8 %collective-permute-start.31 = (bf16[8,24,768]{2,1,0:T(8,128)(2,1)}, bf16[8,24,768]{2,1,0:T(8,128)(2,1)}, u32[]{:S(2)}, u32[]{:S(2)}) collective-permute-start(bf16[8,24,768]{2,1,0:T(8,128)(2,1)} %get-tuple-element.196), channel_id=1, source_target_pairs={{0,2},{1,3},{2,0},{3,1},{4,6},{5,7},{6,4},{7,5},{8,10},{9,11},{10,... | collective-permute-start | bytes 884744 | tf_op jit(solution)/shard_map/ppermute | solution.py:243
  396.1 31.3 %collective-permute-start.32 = (bf16[8,24,768]{2,1,0:T(8,128)(2,1)}, bf16[8,24,768]{2,1,0:T(8,128)(2,1)}, u32[]{:S(2)}, u32[]{:S(2)}) collective-permute-start(bf16[8,24,768]{2,1,0:T(8,128)(2,1)} %get-tuple-element.195), channel_id=1, source_target_pairs={{0,3},{1,2},{2,1},{3,0},{4,7},{5,6},{6,5},{7,4},{8,11},{9,10},{10,... | collective-permute-start | bytes 884744 | tf_op jit(solution)/shard_map/ppermute | solution.py:243
  (137 other events, 1249.9 us)
Sparse Core Ops, SparseCore 0:
  11.5 62.3 all-gather.2
  76.7 82.6 all-gather.4

commit v3 on v2

--- a/solution.py
+++ b/solution.py
@@ -108,17 +108,18 @@
     return grad_query, grad_key, grad_value
 
 
-def branch_rows_kernel(chunks, flipped, x_ref, g_ref, *refs):
-    weights, (hidden_ref, ggate_ref, gup_ref, grad_ref) = refs[: 2 * chunks], refs[2 * chunks :]
+def branch_rows_kernel(chunks, x_ref, g_ref, *refs):
+    weights = refs[:chunks]
+    hidden_ref, ggate_ref, gup_ref, grad_ref, xt_ref, gt_ref = refs[chunks:]
     x, g = x_ref[...], g_ref[...]
-    out_dot = dot if flipped else dot_nt
+    xt_ref[...] = x.T
+    gt_ref[...] = g.T
     total = None
     for chunk in range(chunks):
-        w_in, w_out = weights[2 * chunk], weights[2 * chunk + 1]
-        size = w_in.shape[2]
+        w = weights[chunk]
+        size = w.shape[2]
         at = pl.ds(chunk * size, size)
-        gate, up = dot(x, w_in[0]), dot(x, w_in[1])
-        grad_hidden = out_dot(g, w_out[...])
+        gate, up, grad_hidden = dot(x, w[0]), dot(x, w[1]), dot(g, w[2])
         sigmoid = 1.0 / (1.0 + jnp.exp(-gate))
         active = gate * sigmoid
         hidden_ref[:, at] = (active * up).astype(LOW)
@@ -126,31 +127,32 @@
         gup = (grad_hidden * active).astype(LOW)
         ggate_ref[:, at] = ggate
         gup_ref[:, at] = gup
-        part = dot_nt(ggate, w_in[0]) + dot_nt(gup, w_in[1])
+        part = dot_nt(ggate, w[0]) + dot_nt(gup, w[1])
         total = part if total is None else total + part
     grad_ref[...] = total.astype(LOW)
 
 
-def branch_rows(x, g, chunks, flipped):
+def branch_rows(x, g, chunks):
     rows, width = x.shape
-    size = chunks[0][0].shape[2]
+    size = chunks[0].shape[2]
     hidden = size * len(chunks)
     block = math.gcd(rows, 256)
     row_spec = pl.BlockSpec((block, width), lambda i: (i, 0))
     hidden_spec = pl.BlockSpec((block, hidden), lambda i: (i, 0))
-    weights = [w for chunk in chunks for w in chunk]
     whole = [
-        pl.BlockSpec(w.shape, functools.partial(lambda n, i: (0,) * n, w.ndim),
-                     pipeline_mode=pl.Buffered(1))
-        for w in weights
+        pl.BlockSpec(w.shape, lambda i: (0, 0, 0), pipeline_mode=pl.Buffered(1)) for w in chunks
     ]
     hidden_type = jax.ShapeDtypeStruct((rows, hidden), LOW)
+    turned_spec = pl.BlockSpec((width, block), lambda i: (0, i))
+    turned_type = jax.ShapeDtypeStruct((width, rows), LOW)
     return pl.pallas_call(
-        functools.partial(branch_rows_kernel, len(chunks), flipped),
+        functools.partial(branch_rows_kernel, len(chunks)),
         grid=(rows // block,),
         in_specs=[row_spec, row_spec] + whole,
-        out_specs=[hidden_spec] * 3 + [row_spec],
-        out_shape=[hidden_type] * 3 + [jax.ShapeDtypeStruct((rows, width), LOW)],
+        out_specs=[hidden_spec] * 3 + [row_spec] + [turned_spec] * 2,
+        out_shape=[hidden_type] * 3
+        + [jax.ShapeDtypeStruct((rows, width), LOW)]
+        + [turned_type] * 2,
         compiler_params=pltpu.CompilerParams(vmem_limit_bytes=48 * 1024 * 1024),
         cost_estimate=pl.CostEstimate(
             flops=10 * rows * width * hidden,
@@ -158,31 +160,33 @@
             transcendentals=rows * hidden,
         ),
         name="branch_rows",
-    )(x, g, *weights)
-
-
-def branch_out_kernel(chunks, flipped, hidden_ref, *refs):
+    )(x, g, *chunks)
+
+
+def branch_out_kernel(chunks, hidden_ref, *refs):
     weights, out_ref = refs[:chunks], refs[chunks]
     total = None
     for chunk in range(chunks):
-        w_out = weights[chunk][...]
-        size = w_out.shape[1 if flipped else 0]
-        part = hidden_ref[:, pl.ds(chunk * size, size)]
-        part = dot_nt(part, w_out) if flipped else dot(part, w_out)
+        w_out = weights[chunk][0]
+        size = w_out.shape[1]
+        part = dot_nt(hidden_ref[:, pl.ds(chunk * size, size)], w_out)
         total = part if total is None else total + part
     out_ref[...] = total.astype(LOW)
 
 
-def branch_out(hidden, outs, flipped):
+def branch_out(hidden, chunks):
     rows, size = hidden.shape
-    width = outs[0].shape[0 if flipped else 1]
+    width = chunks[0].shape[1]
     block = math.gcd(rows, 256)
     return pl.pallas_call(
-        functools.partial(branch_out_kernel, len(outs), flipped),
+        functools.partial(branch_out_kernel, len(chunks)),
         grid=(rows // block,),
         in_specs=[pl.BlockSpec((block, size), lambda i: (i, 0))]
         + [
-            pl.BlockSpec(w.shape, lambda i: (0, 0), pipeline_mode=pl.Buffered(1)) for w in outs
+            pl.BlockSpec(
+                (1,) + w.shape[1:], lambda i: (2, 0, 0), pipeline_mode=pl.Buffered(1)
+            )
+            for w in chunks
         ],
         out_specs=pl.BlockSpec((block, width), lambda i: (i, 0)),
         out_shape=jax.ShapeDtypeStruct((rows, width), LOW),
@@ -193,33 +197,27 @@
             transcendentals=0,
         ),
         name="branch_out",
-    )(hidden, *outs)
-
-
-def branch_grads_kernel(x_ref, g_ref, hidden_ref, ggate_ref, gup_ref, in_ref, out_ref):
-    x, g = x_ref[...], g_ref[...]
-    in_ref[0, 0] = dot_tn(x, ggate_ref[...]).astype(LOW)
-    in_ref[0, 1] = dot_tn(x, gup_ref[...]).astype(LOW)
-    out_ref[0] = dot_tn(g, hidden_ref[...]).astype(LOW)
-
-
-def branch_grads(x, g, hidden, ggate, gup, first, chunks, size):
-    rows, width = x.shape
+    )(hidden, *chunks)
+
+
+def branch_grads_kernel(xt_ref, gt_ref, hidden_ref, ggate_ref, gup_ref, grad_ref):
+    xt = xt_ref[...]
+    grad_ref[0, 0] = dot(xt, ggate_ref[...]).astype(LOW)
+    grad_ref[0, 1] = dot(xt, gup_ref[...]).astype(LOW)
+    grad_ref[0, 2] = dot(gt_ref[...], hidden_ref[...]).astype(LOW)
+
+
+def branch_grads(turned, states, first, chunks, size):
+    width, rows = turned[0].shape
     block = math.gcd(width, 256)
-    row_spec = pl.BlockSpec((rows, block), lambda j, i: (0, i))
+    turned_spec = pl.BlockSpec((block, rows), lambda j, i: (i, 0))
     hidden_spec = pl.BlockSpec((rows, size), lambda j, i: (0, first + j))
     return pl.pallas_call(
         branch_grads_kernel,
         grid=(chunks, width // block),
-        in_specs=[row_spec, row_spec, hidden_spec, hidden_spec, hidden_spec],
-        out_specs=[
-            pl.BlockSpec((1, 2, block, size), lambda j, i: (j, 0, i, 0)),
-            pl.BlockSpec((1, block, size), lambda j, i: (j, i, 0)),
-        ],
-        out_shape=[
-            jax.ShapeDtypeStruct((chunks, 2, width, size), LOW),
-            jax.ShapeDtypeStruct((chunks, width, size), LOW),
-        ],
+        in_specs=[turned_spec] * 2 + [hidden_spec] * 3,
+        out_specs=pl.BlockSpec((1, 3, block, size), lambda j, i: (j, 0, i, 0)),
+        out_shape=jax.ShapeDtypeStruct((chunks, 3, width, size), LOW),
         compiler_params=pltpu.CompilerParams(vmem_limit_bytes=48 * 1024 * 1024),
         cost_estimate=pl.CostEstimate(
             flops=6 * rows * width * size * chunks,
@@ -227,7 +225,27 @@
             transcendentals=0,
         ),
         name="branch_grads",
-    )(x, g, hidden, ggate, gup)
+    )(*turned, *states)
+
+
+def sum_turned_kernel(*refs):
+    total = refs[0][0].astype(FULL)
+    for ref in refs[1:-1]:
+        total = total + ref[0].astype(FULL)
+    refs[-1][...] = total.T
+
+
+def sum_turned(parts):
+    _, width, size = parts[0].shape
+    block = math.gcd(width, 256)
+    return pl.pallas_call(
+        sum_turned_kernel,
+        grid=(width // block,),
+        in_specs=[pl.BlockSpec((1, block, size), lambda i: (2, i, 0))] * len(parts),
+        out_specs=pl.BlockSpec((size, block), lambda i: (0, i)),
+        out_shape=jax.ShapeDtypeStruct((size, width), FULL),
+        name="sum_turned",
+    )(*parts)
 
 
 def adam_step(weight, mean_old, square_old, gradient, rate):
@@ -281,18 +299,45 @@
     return total
 
 
-def sum_halving(parts, axis, count):
-    parts = dict(enumerate(parts))
-    mask = 1
-    while mask < count:
-        leaving = [m for m in parts if m & mask]
-        sent = jnp.stack([parts[m].astype(LOW) for m in leaving])
-        got = swap(sent, axis, mask, count).astype(FULL)
-        parts = {
-            m ^ mask: parts[m ^ mask].astype(FULL) + got[at] for at, m in enumerate(leaving)
-        }
-        mask *= 2
-    return parts[0].astype(FULL)
+def axis_bit(axis, mask):
+    return (lax.axis_index(axis) // mask) % 2
+
+
+def masks_of(count):
+    return [1 << bit for bit in reversed(range(count.bit_length() - 1))]
+
+
+def gather_doubling(value, axes, *earlier):
+    steps = [(axis, mask, size) for axis, size in axes for mask in masks_of(size)]
+    rest = value.ndim
+    for axis, mask, size in steps:
+        sent = after(value, *earlier) if earlier else value
+        earlier = ()
+        got = swap(sent, axis, mask, size)
+        low_half = axis_bit(axis, mask) == 0
+        value = jnp.stack([jnp.where(low_half, value, got), jnp.where(low_half, got, value)])
+    order = tuple(reversed(range(len(steps))))
+    value = value.transpose(order + tuple(len(steps) + dim for dim in range(rest)))
+    return value.reshape((-1,) + value.shape[len(steps) :])
+
+
+def sum_step(value, axis, mask, size, dim, *earlier):
+    bit = axis_bit(axis, mask)
+    kept = lax.dynamic_index_in_dim(value, bit, dim, False)
+    sent = lax.dynamic_index_in_dim(value, 1 - bit, dim, False).astype(LOW)
+    if earlier:
+        sent = after(sent, *earlier)
+    return kept.astype(FULL) + swap(sent, axis, mask, size).astype(FULL)
+
+
+def sum_wide(value, wide):
+    place = lax.axis_index("wide")
+    parts = [lax.dynamic_index_in_dim(value, place ^ m, 0, False) for m in range(wide)]
+    got = [swap(parts[m].astype(LOW), "wide", m, wide) for m in range(1, wide)]
+    total = parts[0].astype(FULL)
+    for part in got:
+        total = total + part.astype(FULL)
+    return total
 
 
 def block_of(value, place, size, dim=0):
@@ -350,31 +395,43 @@
     cut = cut.reshape(count, rows_weight, 3 * head_width)
     gain_columns = jnp.broadcast_to(norm_gains.astype(LOW).T[None], (count, rows_weight, 2))
     cut = jnp.concatenate([cut, gain_columns], axis=2)
-    sent = jnp.broadcast_to(cut[None], (wide,) + cut.shape).reshape(
-        wide * count, rows_weight, 3 * head_width + 2
-    )
-    got = lax.all_to_all(sent, ("wide", "tensor"), split_axis=0, concat_axis=0, tiled=True)
+    own_cut = send_relative(
+        [lax.dynamic_index_in_dim(cut, rank ^ m, 0, False) for m in range(count)]
+    )
+    got = gather_doubling(jnp.stack(by_rank(own_cut, rank)), [("wide", wide)])
     got = got.reshape(width, 3 * head_width + 2)
     w_qkv = got[:, : 3 * head_width]
     gain_pair = got[:, 3 * head_width :].astype(FULL).T
 
-    tokens_all = jnp.concatenate(by_rank(gather_relative(tokens, count), rank), axis=0)
-    w_mix_out = lax.all_gather(
-        mixing_out.astype(LOW), ("wide", "tensor"), axis=0, tiled=True
-    )
+    both = jnp.concatenate([tokens, cotangent], axis=1)
+    both = gather_relative(both, count)
+    tokens_all = jnp.concatenate(by_rank([part[:, :width] for part in both], rank), axis=0)
+    cotangent_rel = jnp.concatenate([part[:, width:] for part in both], axis=0)
     shared_low = jnp.concatenate(
         [shared_in.astype(LOW).transpose(1, 0, 2), shared_out.astype(LOW).T[None]], axis=0
     )
     w_shared = lax.all_gather(shared_low, "wide", axis=1, tiled=True)
-    cotangent_rel = jnp.concatenate(gather_relative(cotangent, count), axis=0)
-    expert_chunks = list(
-        zip(
-            gather_relative(expert_in[0].astype(LOW).transpose(1, 0, 2), count),
-            gather_relative(expert_out[0].astype(LOW), count),
-        )
+    expert_low = jnp.concatenate(
+        [expert_in[0].astype(LOW).transpose(1, 0, 2), expert_out.astype(LOW).transpose(0, 2, 1)],
+        axis=0,
     )
     if count == 4:
-        expert_chunks = [expert_chunks[m] for m in (0, 2, 1, 3)]
+        far = []
+        for plane in range(3):
+            far.append(
+                swap(after(expert_low[plane], far[-1] if far else own_cut[1]), "tensor", 2, count)
+            )
+        far_low = jnp.stack(far)
+        expert_chunks = [expert_low, far_low] + [
+            swap(part, "tensor", 1, count) for part in (expert_low, far_low)
+        ]
+    else:
+        far = [own_cut[1]] * 3
+        expert_chunks = gather_relative(expert_low, count)
+    w_mix_out = gather_doubling(
+        mixing_out.astype(LOW), [("wide", wide), ("tensor", count)], own_cut[1]
+    )
+    w_mix_out = w_mix_out.reshape(width, width)
 
     own_routes = lax.dynamic_slice_in_dim(routes, rank * rows_dev, rows_dev, 0)
     own_logits = lax.dynamic_slice_in_dim(gate_logits, rank * rows_dev, rows_dev, 0)
@@ -391,21 +448,22 @@
     grad_out = cotangent.astype(FULL)
     grad_routes = [(gates[:, k : k + 1] * grad_out).astype(LOW) for k in range(TOP)]
     grad_slots = (dot(picks[0], grad_routes[0]) + dot(picks[1], grad_routes[1])).astype(LOW)
-    grad_slots = after(grad_slots, got)
+    grad_slots = after(grad_slots, own_cut[1])
     expert_grads = exchange(grad_slots.reshape(wide, capacity, width)).reshape(slots, width)
 
     tree_places = jnp.arange(tree_length, dtype=jnp.int32)
     segment, upward, position = tree_layout(parents[0], tree_places)
     allowed = allowed_mask(segment, upward, tree_places)
     cosine, sine = rotary_tables(position.astype(FULL))
-    tree_rows = tokens_all.astype(FULL)
+    tree_rows = after(tokens_all, far[0]).astype(FULL)
     normed_one = (tree_rows * rms_factor(tree_rows) * gain_pair[0]).astype(LOW)
     projected = dot(normed_one, w_qkv).reshape(tree_length, 3, heads_dev, HEAD)
     queries = rotate(projected[:, 0], cosine, sine).astype(LOW)
     keys = rotate(projected[:, 1], cosine, sine).astype(LOW)
     values = projected[:, 2].astype(LOW)
     attended, log_totals = attend_forward(queries, keys, values, allowed)
-    attended = after(attended.astype(LOW).reshape(tree_length, head_width), *expert_chunks[1])
+    attended = attended.astype(LOW).reshape(tree_length, head_width)
+    attended = after(attended, expert_grads, far[1])
     attended = send_relative([block_of(attended, rank ^ m, rows_dev) for m in range(count)])
     attended_low = jnp.concatenate(by_rank(attended, rank), axis=1)[:, :width]
     input_rows = tokens.astype(FULL)
@@ -414,51 +472,39 @@
     normed_two = (residual * factor_two * gain_pair[1]).astype(LOW)
 
     row_slots = dot(pick_any, normed_two).astype(LOW)
-    row_slots = after(row_slots, expert_grads)
+    row_slots = after(row_slots, far[2])
     expert_rows = exchange(row_slots.reshape(wide, capacity, width)).reshape(slots, width)
     shared_rows = jnp.concatenate(gather_relative(normed_two, count), axis=0)
-    shared_chunk = (w_shared[:2], w_shared[2])
-    sh_hidden, sh_ggate, sh_gup, sh_grad_rows = branch_rows(
-        shared_rows, cotangent_rel, [shared_chunk], True
-    )
-    sh_grad_rows = sum_relative(jnp.split(sh_grad_rows, count))
-    sh_part = branch_out(sh_hidden, [shared_chunk[1]], True)
-    sh_size = sh_hidden.shape[1]
-    sh_grad_in, sh_grad_out = branch_grads(
-        shared_rows, cotangent_rel, sh_hidden, sh_ggate, sh_gup, 0, 1, sh_size
-    )
-
-    ex_hidden, ex_ggate, ex_gup, ex_grad_rows = branch_rows(
-        expert_rows, expert_grads, expert_chunks, False
-    )
+    *sh_states, sh_grad_rows, sh_xt, sh_gt = branch_rows(shared_rows, cotangent_rel, [w_shared])
+    sh_part = branch_out(sh_states[0], [w_shared])
+    sh_sums = jnp.concatenate([sh_grad_rows, sh_part], axis=1)
+    sh_sums = sum_relative(jnp.split(sh_sums, count))
+    sh_size = sh_states[0].shape[1]
+    sh_grads = branch_grads((sh_xt, sh_gt), sh_states, 0, 1, sh_size)
+    halves = masks_of(wide)
+    sh_grads = sh_grads.reshape((3,) + (2,) * len(halves) + (width // wide, sh_size))
+    sh_grads = sum_step(sh_grads, "wide", halves[-1], wide, len(halves))
+
+    *ex_states, ex_grad_rows, ex_xt, ex_gt = branch_rows(expert_rows, expert_grads, expert_chunks)
     back_rows = exchange(ex_grad_rows.reshape(wide, capacity, width)).reshape(slots, width)
-    out_rows = branch_out(ex_hidden, [chunk[1] for chunk in expert_chunks], False)
-    out_rows = after(out_rows, back_rows)
+    for level in range(len(halves) - 2, 0, -1):
+        sh_grads = sum_step(sh_grads, "wide", halves[level], wide, level + 1, ex_grad_rows)
+    ex_size = ex_states[0].shape[1] // count
+    ex_grads = functools.partial(branch_grads, (ex_xt, ex_gt), ex_states)
+    if count == 4:
+        ex_sent = swap(ex_grads(2, 2, ex_size), "tensor", 1, count)
+        ex_kept = ex_grads(0, 2, ex_size)
+    else:
+        ex_sent, ex_kept = (), ex_grads(0, count, ex_size)
+    out_rows = branch_out(ex_states[0], expert_chunks)
+    back_rows, out_rows, ex_kept = lax.optimization_barrier((back_rows, out_rows, ex_kept))
     returned = exchange(out_rows.reshape(wide, capacity, width)).reshape(slots, width)
-    ex_size = ex_hidden.shape[1] // count
-    ex_grads = functools.partial(
-        branch_grads, expert_rows, expert_grads, ex_hidden, ex_ggate, ex_gup
-    )
-    if count == 4:
-        sent = [swap(part, "tensor", 1, count).astype(FULL) for part in ex_grads(2, 2, ex_size)]
-        kept = ex_grads(0, 2, ex_size)
-        across = [
-            swap((part[1] + got[1]).astype(LOW), "tensor", 2, count)
-            for part, got in zip(kept, sent)
-        ]
-        grad_ex_in, grad_ex_out = [
-            part[0] + got[0] + far.astype(FULL) for part, got, far in zip(kept, sent, across)
-        ]
-    else:
-        grad_ex_in, grad_ex_out = [sum_relative(list(part)) for part in ex_grads(0, count, ex_size)]
-    grad_ex_in = grad_ex_in.transpose(1, 0, 2)
-    grad_ex_out = grad_ex_out.T
-
-    grad_normed_two = dot_tn(pick_any, back_rows) + sh_grad_rows
+
+    grad_normed_two = dot_tn(pick_any, back_rows) + sh_sums[:, :width]
     grad_part, hat_two = rms_back(residual, factor_two, gain_pair[1], grad_normed_two)
     gain_two_part = jnp.sum(grad_normed_two * hat_two, axis=0)
     grad_residual = grad_out + grad_part
-    grad_res_low = grad_residual.astype(LOW)
+    grad_res_low = after(grad_residual.astype(LOW), ex_sent)
     w_mix_pad = jnp.pad(w_mix_out, ((0, head_pad * HEAD), (0, 0)))
     grad_attended = send_relative(
         [
@@ -466,17 +512,28 @@
             for m in range(count)
         ]
     )
-    grad_attended = jnp.concatenate(by_rank(grad_attended, rank), axis=0)
-    grad_attended = grad_attended.reshape(tree_length, heads_dev, HEAD)
-    grad_mix_out = dot_tn(attended_low, grad_res_low).reshape(wide, count, rows_weight, width)
-    grad_mix_out = sum_relative(
-        [lax.dynamic_index_in_dim(grad_mix_out, rank ^ m, 1, False) for m in range(count)]
-    )
-    grad_mix_out = after(grad_mix_out.astype(LOW), returned)
-    grad_mix_out = jnp.sum(exchange(grad_mix_out).astype(FULL), axis=0)
+    grad_attended = lax.optimization_barrier(grad_attended)
+    grad_attended_all = jnp.concatenate(by_rank(grad_attended, rank), axis=0)
+    grad_attended_all = grad_attended_all.reshape(tree_length, heads_dev, HEAD)
+    grad_mix_out = dot_tn(attended_low, grad_res_low)
+    halves_tensor = masks_of(count)
+    grad_mix_out = grad_mix_out.reshape(
+        (2,) * (len(halves) + len(halves_tensor)) + (rows_weight, width)
+    )
+    for level in range(len(halves_tensor) - 1, -1, -1):
+        grad_mix_out = sum_step(
+            grad_mix_out, "tensor", halves_tensor[level], count, len(halves) + level,
+            grad_attended[0],
+        )
+    across = ()
+    if count == 4:
+        across = ex_kept[1].astype(FULL) + ex_sent[1].astype(FULL)
+        across = after(across.astype(LOW), grad_attended[0], grad_mix_out)
+        across = [swap(across[0], "tensor", 2, count), across]
+    sh_grads = sum_step(sh_grads, "wide", halves[0], wide, 1, grad_attended[0])
 
     grad_query, grad_key, grad_value = attend_backward(
-        queries, keys, values, allowed, grad_attended, log_totals
+        queries, keys, values, allowed, grad_attended_all, log_totals
     )
     grad_projected = jnp.stack(
         [rotate(grad_query, cosine, -sine), rotate(grad_key, cosine, -sine), grad_value], axis=1
@@ -487,6 +544,21 @@
         [block_of(grad_normed_one, rank ^ m, rows_dev) for m in range(count)]
     )
     grad_mix_in = dot_tn(normed_one, grad_projected).astype(LOW)
+    grad_mix_in = after(grad_mix_in, *across[:1])
+    returned, sh_sums, sh_grads, grad_mix_out, ex_kept, ex_sent, across = lax.optimization_barrier(
+        (returned, sh_sums, sh_grads, grad_mix_out, ex_kept, ex_sent, across, grad_projected)
+    )[:7]
+    for level in range(len(halves) - 1, -1, -1):
+        grad_mix_out = sum_step(grad_mix_out, "wide", halves[level], wide, level)
+    if count == 4:
+        second = swap(after(across[1][1], across[0]), "tensor", 2, count)
+        third = swap(after(across[1][2], second), "tensor", 2, count)
+        across = jnp.stack([across[0], second, third])
+        ex_parts = [ex_kept[0], ex_sent[0], across]
+    else:
+        ex_parts = send_relative([ex_kept[m] for m in range(count)])
+    grad_ex_in = sum(part[:2].astype(FULL) for part in ex_parts).transpose(1, 0, 2)
+    grad_ex_out = sum_turned(ex_parts)
     sent = jnp.concatenate([grad_mix_in, gain_two_part.astype(LOW)[:, None]], axis=1)
     got = lax.all_to_all(
         sent.reshape(wide * count, rows_weight, 3 * head_width + 1),
@@ -507,17 +579,10 @@
     input_grad = grad_residual + grad_part
 
     per_route = [dot_tn(picks[k], returned) for k in range(TOP)]
-    sh_part = sum_relative(jnp.split(sh_part, count))
-    mixed = residual + gates[:, :1] * per_route[0] + gates[:, 1:] * per_route[1] + sh_part
+    mixed = residual + gates[:, :1] * per_route[0] + gates[:, 1:] * per_route[1]
+    mixed = mixed + sh_sums[:, width:]
     gate_grad = jnp.stack([jnp.sum(grad_out * rows, axis=-1) for rows in per_route], axis=1)
     logit_grad = gates * (gate_grad - jnp.sum(gates * gate_grad, axis=-1, keepdims=True))
-
-    tree = lax.axis_index("wide")
-    rows_shared = width // wide
-    sh_grads = jnp.concatenate([sh_grad_in[0], sh_grad_out], axis=0)
-    sh_grads = sum_halving(
-        [block_of(sh_grads, tree ^ m, rows_shared, 1) for m in range(wide)], "wide", wide
-    )
 
     weights = (mixing_in, mixing_out, norm_gains, shared_in, shared_out, expert_in, expert_out)
     means = (

time: 494 us -> 476 us (0.964)
  the two profiles are of different devices: /device:TPU:3 before, /device:TPU:0 now
where the time goes in v3:
time: 476 us; the launch traced here: 469 us
  waiting for transfers between devices  142 us (30%)
  other arithmetic  75.6 us (16%)
  Pallas kernels  73.8 us (16%)
  starting transfers between devices  66.6 us (14%)
  local copies, waits for them, and re-layouts  51.3 us (11%)
  matrix products  43.1 us (9%)
  between operations  16.5 us (3%)
    ppermute x46, waiting for transfers between devices, swap(): return lax.ppermute(value, axis, [(i, i ^ mask) for i in range(count)])  118 us
    ppermute x46, starting transfers between devices, swap(): return lax.ppermute(value, axis, [(i, i ^ mask) for i in range(count)])  44.8 us
    pallas_call x2, Pallas kernels, branch_rows(): pl.pallas_call(functools.partial(branch_rows_kernel, len(chunks)), grid=(...  34 us
    unnamed x259, local copies, waits for them, and re-layouts  27.2 us
    pallas_call x3, Pallas kernels, branch_grads(): pl.pallas_call(branch_grads_kernel, grid=(chunks, width // block), in_spe...  27 us
    all_to_all x4, waiting for transfers between devices, exchange(): lax.all_to_all(value, 'wide', split_axis=0, concat_axis=0, tiled=True)  23.8 us
    all_to_all x4, starting transfers between devices, exchange(): lax.all_to_all(value, 'wide', split_axis=0, concat_axis=0, tiled=True)  17.9 us
    sub x7, other arithmetic, adam_step(): weight - rate * (mean_hat / (jnp.sqrt(square_hat) + ADAM_EPS) + DECAY * w...  13.8 us
  transfers between devices with their start and end apart: 52, of which 21 were waited for; matrix products, arithmetic and copies ran while one was open for 32% of the time, Pallas kernels for 16%

profile of v3, /device:TPU:0, one launch (start us, length us, event | category | flops | bytes accessed | tf_op | source)
XLA Modules:
  0.0 469.0 jit_solution(6838902964725736067)
XLA Ops:
  47.1 4.9 %collective-permute-done.8 = bf16[2,4,24,578]{3,2,1,0:T(8,128)(2,1)S(1)} collective-permute-done((bf16[2,4,24,578]{3,2,1,0:T(8,128)(2,1)S(1)}, bf16[2,4,24,578]{3,2,1,0:T(8,128)(2,1)S(1)}, u32[]{:S(2)}, u32[]{:S(2)}) %collective-permute-start.8) | collective-permute-done | bytes 221984 | tf_op jit(solution)/shard_map/ppermute | solution.py:261
  57.5 4.5 all-to-all-start
  63.7 11.0 %collective-permute-done.9 = bf16[2,2,4,24,578]{4,3,2,0,1:T(8,128)(2,1)} collective-permute-done((bf16[2,2,4,24,578]{4,3,2,0,1:T(8,128)(2,1)}, bf16[2,2,4,24,578]{4,3,2,0,1:T(8,128)(2,1)}, u32[]{:S(2)}, u32[]{:S(2)}) %collective-permute-start.9) | collective-permute-done | bytes 443936 | tf_op jit(solution)/shard_map/ppermute | solution.py:261
  108.3 12.3 %collective-permute-done.19 = bf16[768,512]{1,0:T(8,128)(2,1)S(1)} collective-permute-done((bf16[768,512]{1,0:T(8,128)(2,1)S(1)}, bf16[768,512]{1,0:T(8,128)(2,1)S(1)}, u32[]{:S(2)}, u32[]{:S(2)}) %collective-permute-start.19) | collective-permute-done | bytes 786464 | tf_op jit(solution)/shard_map/ppermute | solution.py:261
  121.5 4.5 all-to-all-start.1
  134.5 10.4 %collective-permute-done.23 = bf16[256,768]{1,0:T(8,128)(2,1)} collective-permute-done((bf16[256,768]{1,0:T(8,128)(2,1)}, bf16[256,768]{1,0:T(8,128)(2,1)}, u32[]{:S(2)}, u32[]{:S(2)}) %collective-permute-start.23) | collective-permute-done | bytes 393248 | tf_op jit(solution)/shard_map/ppermute | solution.py:261
  149.8 22.9 %all-to-all-done.1 = bf16[8,128,768]{2,1,0:T(8,128)(2,1)} async-done(((bf16[8,128,768]{2,1,0:T(8,128)(2,1)}), bf16[8,128,768]{2,1,0:T(8,128)(2,1)}, u32[]{:S(2)}, u32[]{:S(2)}) %all-to-all-start.1) | async-done | bytes 1572896 | tf_op jit(solution)/shard_map/all_to_all | solution.py:348
  172.7 25.2 %branch_rows.2 = (bf16[1024,2048]{1,0:T(8,128)(2,1)}, bf16[1024,2048]{1,0:T(8,128)(2,1)}, bf16[1024,2048]{1,0:T(8,128)(2,1)}, bf16[1024,768]{1,0:T(8,128)(2,1)S(...) custom-call(bf16[1024,768]{1,0:T(8,128)(2,1)} %bitcast.57.x_ref, bf16[1024,768]{1,0:T(8,128)(2,1)} %bitcast.35.g_ref, ...), custom_call_target="tpu_custom_call" | custom-call | flops 16106127360 | bytes 26738688 | tf_op jit(solution)/shard_map/branch_rows/pallas_call | solution.py:148
  197.9 11.4 %branch_grads.5 = bf16[2,3,768,512]{3,2,1,0:T(8,128)(2,1)} custom-call(bf16[768,1024]{1,0:T(8,128)(2,1)S(1)} %get-tuple-element.78.xt_ref, bf16[768,1024]{1,0:T(8,128)(2,1)S(1)} %get-tuple-element.79.gt_ref, bf16[1024,2048]{1,0:T(8,128)(2,1)} %get-tuple-element.77.hidden_ref, bf16[1024,2048]{1,0:T(8,128)(2,1)} %get-tuple-element.80.ggate_ref, ...), custom_call_target="tpu_custom_call" | custom-call | flops 4831838208 | bytes 20447232 | tf_op jit(solution)/shard_map/branch_grads/pallas_call | solution.py:215
  209.4 8.8 %branch_rows.3 = (bf16[1024,512]{1,0:T(8,128)(2,1)S(1)}, bf16[1024,512]{1,0:T(8,128)(2,1)S(1)}, bf16[1024,512]{1,0:T(8,128)(2,1)S(1)}, bf16[1024,768]{1,0:T(8,12...) custom-call(bf16[1024,768]{1,0:T(8,128)(2,1)} %pad_maximum_fusion.4.x_ref, ...), custom_call_target="tpu_custom_call" | custom-call | flops 4026531840 | bytes 10223616 | tf_op jit(solution)/shard_map/branch_rows/pallas_call | solution.py:148
  223.5 5.2 %branch_grads.4 = bf16[1,3,768,512]{3,2,1,0:T(8,128)(2,1)} custom-call(bf16[768,1024]{1,0:T(8,128)(2,1)S(1)} %copy-done.9, bf16[768,1024]{1,0:T(8,128)(2,1)} %get-tuple-element.86.gt_ref, bf16[1024,512]{1,0:T(8,128)(2,1)S(1)} %get-tuple-element.84.hidden_ref, bf16[1024,512]{1,0:T(8,128)(2,1)S(1)} %get-tuple-element.87.ggate_ref, ...), custom_call_target="tpu_custom_call" | custom-call | flops 2415919104 | bytes 10223616 | tf_op jit(solution)/shard_map/branch_grads/pallas_call | solution.py:215
  235.4 4.5 all-to-all-start.2
  242.9 15.8 %collective-permute-done.26 = bf16[256,1536]{1,0:T(8,128)(2,1)} collective-permute-done((bf16[256,1536]{1,0:T(8,128)(2,1)}, bf16[256,1536]{1,0:T(8,128)(2,1)}, u32[]{:S(2)}, u32[]{:S(2)}) %collective-permute-start.26) | collective-permute-done | bytes 786464 | tf_op jit(solution)/shard_map/ppermute | solution.py:261
  262.0 12.5 %collective-permute-done.28 = bf16[3,2,2,96,512]{4,3,0,1,2:T(8,128)(2,1)} collective-permute-done((bf16[3,2,2,96,512]{4,3,0,1,2:T(8,128)(2,1)}, bf16[3,2,2,96,512]{4,3,0,1,2:T(8,128)(2,1)}, u32[]{:S(2)}, u32[]{:S(2)}) %collective-permute-start.28) | collective-permute-done | bytes 1179680 | tf_op jit(solution)/shard_map/ppermute | solution.py:261
  276.6 7.3 %branch_out.2 = bf16[1024,768]{1,0:T(8,128)(2,1)} custom-call(bf16[1024,2048]{1,0:T(8,128)(2,1)} %get-tuple-element.77.hidden_ref, bf16[3,768,512]{2,1,0:T(8,128)(2,1)S(1)} %copy-done.3, bf16[3,768,512]{2,1,0:T(8,128)(2,1)} %pad_maximum_fusion.1.refs_1_, bf16[3,768,512]{2,1,0:T(8,128)(2,1)} %collective-permute-done.20.refs_2_, ...), custom_call_target="tpu_custom_call" | custom-call | flops 3221225472 | bytes 8912896 | tf_op jit(solution)/shard_map/branch_out/pallas_call | solution.py:181
  283.8 10.4 %branch_grads.3 = bf16[2,3,768,512]{3,2,1,0:T(8,128)(2,1)} custom-call(bf16[768,1024]{1,0:T(8,128)(2,1)S(1)} %get-tuple-element.78.xt_ref, bf16[768,1024]{1,0:T(8,128)(2,1)S(1)} %copy-done.5, bf16[1024,2048]{1,0:T(8,128)(2,1)} %get-tuple-element.77.hidden_ref, bf16[1024,2048]{1,0:T(8,128)(2,1)} %get-tuple-element.80.ggate_ref, ...), custom_call_target="tpu_custom_call" | custom-call | flops 4831838208 | bytes 20447232 | tf_op jit(solution)/shard_map/branch_grads/pallas_call | solution.py:215
  295.2 4.4 all-to-all-start.3
  315.6 6.8 %fusion.25 = bf16[1024,1,3,64]{0,3,2,1:T(8,128)(2,1)S(1)} fusion(bf16[1024,3,64]{0,2,1:T(8,128)(2,1)S(1)} %bitcast.290, f32[3,1024,1024]{1,2,0:T(8,128)} %copy-done.10, f32[3,1024]{1,0:T(4,128)S(1)} %copy-done.54), kind=kOutput, calls=%fused_computation.73 | convolution fusion | flops 409141248 | bytes 13381632 | tf_op jit(solution)/shard_map/hqk,qhd->khd/dot_general | solution.py:105
  326.1 5.5 %multiply_convert_fusion = bf16[3,1024,1024]{1,2,0:T(8,128)(2,1)} fusion(f32[3,1024,1024]{1,2,0:T(8,128)S(1)} %get-tuple-element.317, f32[3,1024,1024]{1,2,0:T(8,128)S(1)} %bitcast.278, f32[3,1024]{1,0:T(4,128)S(1)} %get-tuple-element.316, f32[3,1024]{1,0:T(4,128)S(1)} %copy-done.54), kind=kLoop, calls=%fused_computation | loop fusion | flops 12582912 | bytes 31481856 | tf_op jit(solution)/shard_map/convert_element_type | solution.py:102
  331.7 5.0 %fusion.19 = f32[1024,3,64]{0,2,1:T(8,128)S(1)} fusion(bf16[3,1024,1024]{1,2,0:T(8,128)(2,1)} %multiply_convert_fusion, bf16[1024,3,32]{0,2,1:T(8,128)(2,1)S(1)} %copy-done.68, bf16[1024,3,32]{0,2,1:T(8,128)(2,1)S(1)} %copy-done.66), kind=kOutput, calls=%fused_computation.66 | convolution fusion | flops 403636224 | bytes 7471104 | tf_op jit(solution)/shard_map/hqk,qhd->khd/dot_general | solution.py:104
  350.2 20.5 %collective-permute-done.36 = bf16[2,2,2,24,768]{4,3,0,1,2:T(8,128)(2,1)S(1)} collective-permute-done((bf16[2,2,2,24,768]{4,3,0,1,2:T(8,128)(2,1)S(1)}, bf16[2,2,2,24,768]{4,3,0,1,2:T(8,128)(2,1)S(1)}, u32[]{:S(2)}, u32[]{:S(2)}) %collective-permute-start.36) | collective-permute-done | bytes 294944 | tf_op jit(solution)/shard_map/ppermute | solution.py:261
  376.9 14.9 %collective-permute-done.37 = bf16[768,512]{1,0:T(8,128)(2,1)S(1)} collective-permute-done((bf16[768,512]{1,0:T(8,128)(2,1)S(1)}, bf16[768,512]{1,0:T(8,128)(2,1)S(1)}, u32[]{:S(2)}, u32[]{:S(2)}) %collective-permute-start.37) | collective-permute-done | bytes 786464 | tf_op jit(solution)/shard_map/ppermute | solution.py:261
  429.3 4.8 %multiply_subtract_fusion = (f32[1,768,2,512]{3,1,2,0:T(8,128)S(1)}, f32[1,768,2,512]{3,1,2,0:T(8,128)S(1)}, f32[1,768,2,512]{3,1,2,0:T(8,128)S(1)}) fusion(f32[1,768,2,512]{3,2,1,0:T(2,128)S(1)} %copy-done.15, bf16[1,768,512]{2,1,0:T(8,128)(2,1)S(1)} %bitcast.296, bf16[1,768,512]{2,1,0:T(8,128)(2,1)S(1)} %bitcast.294, ...), kind=kLoop, calls=%fused_computation.34 | loop fusion | flops 15728640 | bytes 23592960 | tf_op jit(solution)/shard_map/sub | solution.py:256
  453.5 5.4 %multiply_subtract_fusion.1 = (f32[1,512,768]{2,1,0:T(8,128)}, f32[1,512,768]{2,1,0:T(8,128)}, f32[1,512,768]{2,1,0:T(8,128)}) fusion(f32[1,512,768]{2,1,0:T(8,128)S(1)} %copy-done.26, f32[512,768]{1,0:T(8,128)} %sum_turned.1, f32[1,512,768]{2,1,0:T(8,128)} %param.51, f32[1,512,768]{2,1,0:T(8,128)} %param.50), kind=kLoop, calls=%fused_computation.57 | loop fusion | flops 5505024 | bytes 11010048 | tf_op jit(solution)/shard_map/sub | solution.py:256
  (496 shorter events, 213.5 us)
Async XLA Ops:
  10.9 69.3 %collective-permute-start.2 = (bf16[256,1536]{1,0:T(8,128)(2,1)}, bf16[256,1536]{1,0:T(8,128)(2,1)}, u32[]{:S(2)}, u32[]{:S(2)}) collective-permute-start(bf16[256,1536]{1,0:T(8,128)(2,1)} %constant_dynamic-update-slice_fusion), channel_id=1, source_target_pairs={{0,1},{1,0},{2,3},{3,2},{4,5},{5,4},{6,7},{7,6},{8,9},{9,8},{10,11... | collective-permute-start | bytes 2359304 | tf_op jit(solution)/shard_map/ppermute | solution.py:261
  11.4 51.8 %collective-permute-start = (bf16[256,1536]{1,0:T(8,128)(2,1)}, bf16[256,1536]{1,0:T(8,128)(2,1)}, u32[]{:S(2)}, u32[]{:S(2)}) collective-permute-start(bf16[256,1536]{1,0:T(8,128)(2,1)} %constant_dynamic-update-slice_fusion), channel_id=1, source_target_pairs={{0,2},{1,3},{2,0},{3,1},{4,6},{5,7},{6,4},{7,5},{8,10},{9,11},{10,... | collective-permute-start | bytes 2359304 | tf_op jit(solution)/shard_map/ppermute | solution.py:261
  52.9 21.8 %collective-permute-start.9 = (bf16[2,2,4,24,578]{4,3,2,0,1:T(8,128)(2,1)}, bf16[2,2,4,24,578]{4,3,2,0,1:T(8,128)(2,1)}, u32[]{:S(2)}, u32[]{:S(2)}) collective-permute-start(bf16[2,2,4,24,578]{4,3,2,0,1:T(8,128)(2,1)} %pad_maximum_fusion.13), channel_id=1, source_target_pairs={{0,4},{4,0},{8,12},{12,8},{16,20},{20,16},{24,28},{28,24},{1,5},{5... | collective-permute-start | bytes 1331720 | tf_op jit(solution)/shard_map/ppermute | solution.py:261
  56.0 20.6 %collective-permute-start.4 = (bf16[768,512]{1,0:T(8,128)(2,1)}, bf16[768,512]{1,0:T(8,128)(2,1)}, u32[]{:S(2)}, u32[]{:S(2)}) collective-permute-start(bf16[768,512]{1,0:T(8,128)(2,1)} %get-tuple-element.68), channel_id=1, source_target_pairs={{0,2},{1,3},{2,0},{3,1},{4,6},{5,7},{6,4},{7,5},{8,10},{9,11},{10,... | collective-permute-start | bytes 2359304 | tf_op jit(solution)/shard_map/ppermute | solution.py:261
  57.5 40.0 %all-to-all-start = ((bf16[8,128,768]{2,1,0:T(8,128)(2,1)}), bf16[8,128,768]{2,1,0:T(8,128)(2,1)}, u32[]{:S(2)}, u32[]{:S(2)}) async-start(bf16[8,128,768]{2,1,0:T(8,128)(2,1)} %bitcast.34), calls=%async_computation | async-start | bytes 3145728 | tf_op jit(solution)/shard_map/all_to_all | solution.py:348
  76.6 20.0 %collective-permute-start.10 = (bf16[768,512]{1,0:T(8,128)(2,1)S(1)}, bf16[768,512]{1,0:T(8,128)(2,1)}, u32[]{:S(2)}, u32[]{:S(2)}) collective-permute-start(bf16[768,512]{1,0:T(8,128)(2,1)S(1)} %copy-done.58), channel_id=1, source_target_pairs={{0,2},{1,3},{2,0},{3,1},{4,6},{5,7},{6,4},{7,5},{8,10},{9,11},{10,... | collective-permute-start | bytes 2359304 | tf_op jit(solution)/shard_map/ppermute | solution.py:261
  101.0 19.7 %collective-permute-start.19 = (bf16[768,512]{1,0:T(8,128)(2,1)S(1)}, bf16[768,512]{1,0:T(8,128)(2,1)S(1)}, u32[]{:S(2)}, u32[]{:S(2)}) collective-permute-start(bf16[768,512]{1,0:T(8,128)(2,1)S(1)} %bitcast.298), channel_id=1, source_target_pairs={{0,2},{1,3},{2,0},{3,1},{4,6},{5,7},{6,4},{7,5},{8,10},{9,11},{10,... | collective-permute-start | bytes 2359304 | tf_op jit(solution)/shard_map/ppermute | solution.py:261
  121.5 51.2 %all-to-all-start.1 = ((bf16[8,128,768]{2,1,0:T(8,128)(2,1)}), bf16[8,128,768]{2,1,0:T(8,128)(2,1)}, u32[]{:S(2)}, u32[]{:S(2)}) async-start(bf16[8,128,768]{2,1,0:T(8,128)(2,1)} %bitcast.304), calls=%async_computation.1 | async-start | bytes 3145728 | tf_op jit(solution)/shard_map/all_to_all | solution.py:348
  126.0 83.4 %all-gather.2.cloned.1.call-start = ((), (), s32[]{:S(2)}) async-start(), calls=%async_computation.5 | async-start | bytes 2654208 | tf_op jit(solution)/shard_map/all_gather | solution.py:413
  128.2 21.6 %collective-permute-start.20 = (bf16[3,768,512]{2,1,0:T(8,128)(2,1)S(1)}, bf16[3,768,512]{2,1,0:T(8,128)(2,1)}, u32[]{:S(2)}, u32[]{:S(2)}) collective-permute-start(bf16[3,768,512]{2,1,0:T(8,128)(2,1)S(1)} %pad_maximum_fusion.refs_0_), channel_id=1, source_target_pairs={{0,1},{1,0},{2,3},{3,2},{4,5},{5,4},{6,7},{7,6},{8,9},{9,8},{10,11... | collective-permute-start | bytes 7077896 | tf_op jit(solution)/shard_map/ppermute | solution.py:261
  209.3 96.3 %collective-permute-start.30 = (bf16[2,3,768,512]{3,2,1,0:T(8,128)(2,1)}, bf16[2,3,768,512]{3,2,1,0:T(8,128)(2,1)}, u32[]{:S(2)}, u32[]{:S(2)}) collective-permute-start(bf16[2,3,768,512]{3,2,1,0:T(8,128)(2,1)} %branch_grads.5), channel_id=1, source_target_pairs={{0,1},{1,0},{2,3},{3,2},{4,5},{5,4},{6,7},{7,6},{8,9},{9,8},{10,11... | collective-permute-start | bytes 14155784 | tf_op jit(solution)/shard_map/ppermute | solution.py:261
  221.3 21.6 %collective-permute-start.25 = (bf16[256,1536]{1,0:T(8,128)(2,1)}, bf16[256,1536]{1,0:T(8,128)(2,1)}, u32[]{:S(2)}, u32[]{:S(2)}) collective-permute-start(bf16[256,1536]{1,0:T(8,128)(2,1)} %get-tuple-element.237), channel_id=1, source_target_pairs={{0,1},{1,0},{2,3},{3,2},{4,5},{5,4},{6,7},{7,6},{8,9},{9,8},{10,11... | collective-permute-start | bytes 2359304 | tf_op jit(solution)/shard_map/ppermute | solution.py:261
  221.8 21.2 %collective-permute-start.27 = (bf16[256,1536]{1,0:T(8,128)(2,1)}, bf16[256,1536]{1,0:T(8,128)(2,1)}, u32[]{:S(2)}, u32[]{:S(2)}) collective-permute-start(bf16[256,1536]{1,0:T(8,128)(2,1)} %get-tuple-element.238), channel_id=1, source_target_pairs={{0,3},{1,2},{2,1},{3,0},{4,7},{5,6},{6,5},{7,4},{8,11},{9,10},{10,... | collective-permute-start | bytes 2359304 | tf_op jit(solution)/shard_map/ppermute | solution.py:261
  222.6 36.1 %collective-permute-start.26 = (bf16[256,1536]{1,0:T(8,128)(2,1)}, bf16[256,1536]{1,0:T(8,128)(2,1)}, u32[]{:S(2)}, u32[]{:S(2)}) collective-permute-start(bf16[256,1536]{1,0:T(8,128)(2,1)} %get-tuple-element.239), channel_id=1, source_target_pairs={{0,2},{1,3},{2,0},{3,1},{4,6},{5,7},{6,4},{7,5},{8,10},{9,11},{10,... | collective-permute-start | bytes 2359304 | tf_op jit(solution)/shard_map/ppermute | solution.py:261
  232.8 41.8 %collective-permute-start.28 = (bf16[3,2,2,96,512]{4,3,0,1,2:T(8,128)(2,1)}, bf16[3,2,2,96,512]{4,3,0,1,2:T(8,128)(2,1)}, u32[]{:S(2)}, u32[]{:S(2)}) collective-permute-start(bf16[3,2,2,96,512]{4,3,0,1,2:T(8,128)(2,1)} %bitcast.272), channel_id=1, source_target_pairs={{0,4},{4,0},{8,12},{12,8},{16,20},{20,16},{24,28},{28,24},{1,5},{5... | collective-permute-start | bytes 3538952 | tf_op jit(solution)/shard_map/ppermute | solution.py:261
  235.4 59.8 %all-to-all-start.2 = ((bf16[8,128,768]{2,1,0:T(8,128)(2,1)}), bf16[8,128,768]{2,1,0:T(8,128)(2,1)}, u32[]{:S(2)}, u32[]{:S(2)}) async-start(bf16[8,128,768]{2,1,0:T(8,128)(2,1)} %bitcast.276), calls=%async_computation.2 | async-start | bytes 3145728 | tf_op jit(solution)/shard_map/all_to_all | solution.py:348
  295.2 96.7 %all-to-all-start.3 = ((bf16[8,128,768]{2,1,0:T(8,128)(2,1)}), bf16[8,128,768]{2,1,0:T(8,128)(2,1)}, u32[]{:S(2)}, u32[]{:S(2)}) async-start(bf16[8,128,768]{2,1,0:T(8,128)(2,1)} %bitcast.63), calls=%async_computation.3 | async-start | bytes 3145728 | tf_op jit(solution)/shard_map/all_to_all | solution.py:348
  338.0 36.1 %collective-permute-start.34 = (bf16[3,96,512]{2,1,0:T(8,128)(2,1)S(1)}, bf16[3,96,512]{2,1,0:T(8,128)(2,1)S(1)}, u32[]{:S(2)}, u32[]{:S(2)}) collective-permute-start(bf16[3,96,512]{2,1,0:T(8,128)(2,1)S(1)} %copy-done.82), channel_id=1, source_target_pairs={{0,16},{4,20},{8,24},{12,28},{16,0},{20,4},{24,8},{28,12},{1,17},{... | collective-permute-start | bytes 884744 | tf_op jit(solution)/shard_map/ppermute | solution.py:261
  344.3 30.7 %collective-permute-start.38 = (bf16[256,768]{1,0:T(8,128)(2,1)S(1)}, bf16[256,768]{1,0:T(8,128)(2,1)S(1)}, u32[]{:S(2)}, u32[]{:S(2)}) collective-permute-start(bf16[256,768]{1,0:T(8,128)(2,1)S(1)} %get-tuple-element.251), channel_id=1, source_target_pairs={{0,1},{1,0},{2,3},{3,2},{4,5},{5,4},{6,7},{7,6},{8,9},{9,8},{10,11... | collective-permute-start | bytes 1179656 | tf_op jit(solution)/shard_map/ppermute | solution.py:261
  344.5 30.5 %collective-permute-start.40 = (bf16[256,768]{1,0:T(8,128)(2,1)S(1)}, bf16[256,768]{1,0:T(8,128)(2,1)S(1)}, u32[]{:S(2)}, u32[]{:S(2)}) collective-permute-start(bf16[256,768]{1,0:T(8,128)(2,1)S(1)} %get-tuple-element.252), channel_id=1, source_target_pairs={{0,3},{1,2},{2,1},{3,0},{4,7},{5,6},{6,5},{7,4},{8,11},{9,10},{10,... | collective-permute-start | bytes 1179656 | tf_op jit(solution)/shard_map/ppermute | solution.py:261
  345.7 29.2 %collective-permute-start.39 = (bf16[256,768]{1,0:T(8,128)(2,1)S(1)}, bf16[256,768]{1,0:T(8,128)(2,1)S(1)}, u32[]{:S(2)}, u32[]{:S(2)}) collective-permute-start(bf16[256,768]{1,0:T(8,128)(2,1)S(1)} %get-tuple-element.253), channel_id=1, source_target_pairs={{0,2},{1,3},{2,0},{3,1},{4,6},{5,7},{6,4},{7,5},{8,10},{9,11},{10,... | collective-permute-start | bytes 1179656 | tf_op jit(solution)/shard_map/ppermute | solution.py:261
  346.7 23.9 %collective-permute-start.36 = (bf16[2,2,2,24,768]{4,3,0,1,2:T(8,128)(2,1)S(1)}, bf16[2,2,2,24,768]{4,3,0,1,2:T(8,128)(2,1)S(1)}, u32[]{:S(2)}, u32[]{:S(2)}) collective-permute-start(bf16[2,2,2,24,768]{4,3,0,1,2:T(8,128)(2,1)S(1)} %fusion.73), channel_id=1, source_target_pairs={{0,2},{1,3},{2,0},{3,1},{4,6},{5,7},{6,4},{7,5},{8,10},{9,11},{10,... | collective-permute-start | bytes 884744 | tf_op jit(solution)/shard_map/ppermute | solution.py:261
  394.6 64.4 %all-to-all-start.4 = ((bf16[32,24,577]{2,1,0:T(8,128)(2,1)}), bf16[32,24,577]{2,1,0:T(8,128)(2,1)S(1)}, u32[]{:S(2)}, u32[]{:S(2)}) async-start(bf16[32,24,577]{2,1,0:T(8,128)(2,1)} %pad_maximum_fusion.10), calls=%async_computation.4 | async-start | bytes 1966080 | tf_op jit(solution)/shard_map/all_to_all | solution.py:563
  403.2 25.4 %collective-permute-start.44 = (bf16[768,512]{1,0:T(8,128)(2,1)S(1)}, bf16[768,512]{1,0:T(8,128)(2,1)S(1)}, u32[]{:S(2)}, u32[]{:S(2)}) collective-permute-start(bf16[768,512]{1,0:T(8,128)(2,1)S(1)} %get-tuple-element.110), channel_id=1, source_target_pairs={{0,2},{1,3},{2,0},{3,1},{4,6},{5,7},{6,4},{7,5},{8,10},{9,11},{10,... | collective-permute-start | bytes 2359304 | tf_op jit(solution)/shard_map/ppermute | solution.py:261
  (152 other events, 1023.5 us)
Sparse Core Ops, SparseCore 0:
  133.2 65.2 all-gather.1
